TPU v7x, 256 devices: a whole 4x4x8 slice. The times are simulated.
256 devices in a mesh: view: 4 (over x_hi, core), patch: 64 (over y, x_lo, z).
Axes of the slice: x: 4 (x_hi: 2, x_lo: 2; x = x_hi * 2 + x_lo), y: 4, z: 8, core: 2. Of those that a mesh axis runs over, the one named last changes fastest.
Arguments:
- queries: bfloat16 [32768, 768], P(('view', 'patch')), may hold values from -6 to 6
- key_rows: bfloat16 [32768, 768], P(('view', 'patch')), may hold values from -6 to 6
- value_rows: bfloat16 [32768, 768], P(('view', 'patch')), may hold values from -6 to 6
- step_rates: float32 [32768, 4], P(('view', 'patch')), may hold values from 0.5 to 18, as said below
- fast_init: float32 [192, 4608], replicated, may hold values from -2.598076 to 2.598076
- out_grad: bfloat16 [32768, 768], P(('view', 'patch')), may hold values from -6 to 6
Outputs:
- query_grad: bfloat16 [32768, 768], P(('view', 'patch'))
- key_grad: bfloat16 [32768, 768], P(('view', 'patch'))
- value_grad: bfloat16 [32768, 768], P(('view', 'patch'))
- rate_grad: float32 [32768, 4], P(('view', 'patch'))
- fast_grad: float32 [192, 4608], P(None, ('view', 'patch'))
Inputs may be any that keep to these rules, and one draw needn't show every extreme that they name: `step_rates`: positive learning rates.
All inputs are finite; a program needn't handle non-finite values.
Results may differ from a plain program's by a relative error of at most 0.0023.
Values sent between devices are 32-bit elements; how exact they have to be, the bound alone decides.
A program may use at most 128 MiB of HBM per device.

v0:
```python
import math

import jax
import jax.numpy as jnp
from jax import lax
from jax.sharding import Mesh
from jax.sharding import PartitionSpec as P

VIEW_PATCH = ("view_0", "view_1", "patch_0", "patch_1", "patch_2")
VIEW = ("view_0", "view_1")
PATCH = ("patch_0", "patch_1", "patch_2")


highest = lax.Precision.HIGHEST
product_precision = lax.Precision.HIGH
step_size = 0.2
epsilon = 1e-06


def by_axis(array, axes):
    for axis in axes:
        array = lax.psum(array, axis)
    return array


def fast_apply(inputs, weights):
    gate_act = jnp.einsum("rhd,dhc->rhc", inputs, weights[:, 0], precision=product_precision)
    up_act = jnp.einsum("rhd,dhc->rhc", inputs, weights[:, 1], precision=product_precision)
    hidden = jax.nn.silu(gate_act) * up_act
    return jnp.einsum("rhc,dhc->rhd", hidden, weights[:, 2], precision=product_precision)


def update_term(key_part, value_part, rate_part, weights):

    def objective(fast):
        return -jnp.sum(rate_part[:, :, None] * value_part * fast_apply(key_part, fast))

    return jax.grad(objective)(weights)


def head_columns(first_col, own_width, heads, hidden_units):
    column_ids = first_col + jnp.arange(own_width, dtype=jnp.int32)
    head_ids = column_ids // hidden_units % heads
    return (head_ids[:, None] == jnp.arange(heads, dtype=jnp.int32)[None, :]).astype(jnp.float32)


def rate_totals(step_rates):
    return by_axis(jnp.sum(step_rates, 0), VIEW_PATCH)


def on_device(queries, key_rows, value_rows, step_rates, fast_init, out_grad):
    row_count = queries.shape[0]
    head_dim, columns = fast_init.shape
    heads = step_rates.shape[1]
    hidden_units = columns // (3 * heads)
    devices = lax.axis_size(VIEW) * lax.axis_size(PATCH)
    coefficient = step_size * math.sqrt(row_count * devices)
    share = columns // devices
    my_first = lax.axis_index(VIEW_PATCH) * share

    def to_heads(tensor):
        return tensor.astype(jnp.float32).reshape(row_count, heads, head_dim)

    def from_heads(tensor):
        return tensor.reshape(row_count, heads * head_dim).astype(jnp.bfloat16)

    weights = fast_init.reshape(head_dim, 3, heads, hidden_units)
    totals = rate_totals(step_rates)
    rate_scale = coefficient / totals
    partial_value, pull_update = jax.vjp(
        update_term, to_heads(key_rows), to_heads(value_rows), step_rates, weights
    )
    flat_terms = partial_value.reshape(head_dim, columns)
    first_col = 0
    summed = lax.psum(flat_terms, VIEW_PATCH)
    owner_map = head_columns(first_col, columns, heads, hidden_units)
    col_scale = jnp.dot(owner_map, rate_scale, precision=highest)
    grad_cols = summed * col_scale[None, :]
    moved = fast_init - grad_cols
    init_norm = jnp.sqrt(jnp.sum(fast_init * fast_init, 0) + epsilon)
    inverse = lax.rsqrt(jnp.sum(moved * moved, 0) + epsilon)
    col_ratio = init_norm * inverse
    renormed = moved * col_ratio
    _, pull_apply = jax.vjp(
        fast_apply, to_heads(queries), renormed.reshape(head_dim, 3, heads, hidden_units)
    )
    query_part, new_part = pull_apply(to_heads(out_grad))
    flat_new = new_part.reshape(head_dim, columns)
    d_new = lax.psum(flat_new, VIEW_PATCH)
    column_dots = jnp.sum(d_new * moved, 0)
    d_moved = d_new * col_ratio - moved * (column_dots * init_norm * inverse * inverse * inverse)
    direct = d_moved + fast_init * (column_dots * inverse / init_norm)
    d_update = -d_moved
    head_part = jnp.dot(jnp.sum(d_update * grad_cols, 0), owner_map, precision=highest)
    d_totals = -head_part / totals
    d_terms = d_update * col_scale[None, :]
    key_part, value_part, rate_part, fast_part = pull_update(
        d_terms.reshape(head_dim, 3, heads, hidden_units)
    )
    rate_grad = rate_part + d_totals[None, :]
    second = lax.psum_scatter(
        fast_part.reshape(head_dim, columns), VIEW_PATCH, scatter_dimension=1, tiled=True
    )
    direct_own = lax.dynamic_slice_in_dim(direct, my_first, share, 1)
    fast_grad = (direct_own + second) / math.sqrt(row_count * devices)
    return (
        from_heads(query_part),
        from_heads(key_part),
        from_heads(value_part),
        rate_grad,
        fast_grad,
    )


def solution(mesh):
    finer = Mesh(
        mesh.devices.reshape(2, 2, 4, 2, 8), ("view_0", "view_1", "patch_0", "patch_1", "patch_2")
    )
    return jax.shard_map(
        on_device,
        mesh=finer,
        in_specs=(
            P(VIEW_PATCH, None),
            P(VIEW_PATCH, None),
            P(VIEW_PATCH, None),
            P(VIEW_PATCH, None),
            P(),
            P(VIEW_PATCH, None),
        ),
        out_specs=(
            P(VIEW_PATCH, None),
            P(VIEW_PATCH, None),
            P(VIEW_PATCH, None),
            P(VIEW_PATCH, None),
            P(None, VIEW_PATCH),
        ),
        check_vma=False,
    )
```

profile of v0, /device:TPU:1, one launch (start us, length us, event | category | flops | bytes accessed | tf_op | source)
XLA Modules:
  0.0 897.9 jit_solution(10367840104814305219)
XLA Ops:
  7.2 1.7 copy.90
  9.0 3.3 reshape.112
  12.3 2.1 fusion.77
  14.4 1.1 copy.88
  15.5 2.5 fusion.8
  18.0 1.5 convolution_bitcast_fusion.9
  19.6 1.0 fusion.74
  20.6 0.6 convolution_bitcast_fusion.8
  21.3 0.8 convolution_bitcast_fusion.1
  22.1 0.7 convolution_bitcast_fusion.7
  23.1 2.3 copy.95
  25.4 3.1 reshape.114
  28.7 5.9 psum.50
  34.6 5.9 psum.51
  40.5 7.4 psum.52
  47.8 4.2 psum.53
  52.0 17.6 %psum.54 = f32[4]{0:T(128)S(1)} all-reduce(f32[4]{0:T(128)S(1)} %psum.53), channel_id=1, replica_groups=mesh['view_0'=2,'view_1'=2,'patch_0'=4,'patch_1'=2,'patch_2'=8] {'patch_2'}, use_global_device_ids=true, to_apply=%region_6.7 | all-reduce | flops 4 | bytes 32 | tf_op jit(solution)/shard_map/psum | solution.py:22
  69.6 0.8 copy.99
  70.4 0.8 copy.97
  71.9 0.8 convolution_reduce_fusion
  72.7 225.0 %all-reduce.14.cloned.1.call-done = f32[192,4608]{1,0:T(8,128)} async-done(((f32[192,4608]{1,0:T(8,128)}), f32[192,4608]{1,0:T(8,128)}) %all-reduce.14.cloned.1.call-update) | async-done | bytes 3538960 | tf_op jit(solution)/shard_map/psum | solution.py:75
  297.7 3.9 multiply_reduce_fusion.2
  302.9 2.2 broadcast_multiply_fusion
  305.1 5.2 reshape.115
  310.3 2.7 fusion.76
  313.0 1.1 fusion.9
  314.1 1.0 fusion.10
  315.2 1.0 fusion.4
  316.3 0.6 convolution_bitcast_fusion.5
  317.1 0.8 convolution_bitcast_fusion.4
  317.9 0.6 convolution_bitcast_fusion.6
  318.8 4.1 copy.102
  322.9 5.4 reshape.118
  328.4 10.6 %all-reduce.18.cloned.1.call-start = ((), (), s32[]{:S(2)}) async-start(), calls=%async_computation.2 | async-start | bytes 7077888
  339.0 2.9 fusion.11
  342.0 1.6 fusion.5
  343.7 1.7 copy.110
  345.4 248.6 %all-reduce.16.cloned.1.call-done = f32[192,4608]{1,0:T(8,128)} async-done(((f32[192,4608]{1,0:T(8,128)}), f32[192,4608]{1,0:T(8,128)}) %all-reduce.16.cloned.1.call-update) | async-done | bytes 3538960 | tf_op jit(solution)/shard_map/psum | solution.py:89
  594.0 2.5 multiply_reduce_fusion.1
  596.5 2.0 rsqrt_multiply_fusion
  598.5 1.8 multiply_reduce_fusion
  600.3 1.8 copy-done
  602.0 2.2 negate_multiply_fusion
  604.2 3.3 reshape.119
  608.5 1.0 fusion.12
  610.5 1.6 fusion.13
  612.2 1.1 fusion.29
  613.4 2.0 multiply_add_fusion
  616.8 0.7 convolution_bitcast_fusion
  617.7 2.3 copy.109
  620.0 3.4 reshape.120
  623.5 1.2 copy-done.7
  624.9 0.8 convolution_bitcast_fusion.12
  626.5 0.8 fusion.3
  628.0 0.7 fusion.6
  628.8 0.8 copy.111
  629.6 0.8 convolution_bitcast_fusion.10
  631.2 0.8 multiply_reduce_fusion.4
  632.1 0.8 copy.112
  632.9 0.8 dynamic-slice.1
  634.0 0.7 broadcast_add_fusion
  634.6 254.5 %all-reduce.18.cloned.1.call-done = f32[192,4608]{1,0:T(8,128)} async-done(((f32[192,4608]{1,0:T(8,128)}), f32[192,4608]{1,0:T(8,128)}) %all-reduce.18.cloned.1.call-update) | async-done | bytes 3538960
  889.1 1.3 fusion.56
  890.4 0.7 copy.113
  (132 shorter events, 9.5 us)
Async XLA Ops:
  7.2 290.6 %all-reduce.14.cloned.1.call-start = ((), (), s32[]{:S(2)}) async-start(), calls=%async_computation | async-start | bytes 7077888 | tf_op jit(solution)/shard_map/psum | solution.py:75
  15.4 5.9 copy-start.13
  15.4 2.5 copy-start.3
  15.5 2.5 copy-start.57
  18.0 3.3 copy-start.22
  18.0 1.5 copy-start.6
  18.0 1.5 copy-start.8
  19.5 1.2 copy-start.25
  20.6 1.5 copy-start.40
  20.6 1.5 copy-start.43
  20.6 1.5 copy-start.45
  28.5 41.1 %copy-start.47 = (bf16[128,768]{1,0:T(8,128)(2,1)S(1)}, bf16[128,768]{1,0:T(8,128)(2,1)}, u32[]{:S(2)}) copy-start(bf16[128,768]{1,0:T(8,128)(2,1)} %param.11) | copy-start | bytes 589828
  28.5 41.9 %copy-start.48 = (bf16[128,768]{1,0:T(8,128)(2,1)S(1)}, bf16[128,768]{1,0:T(8,128)(2,1)}, u32[]{:S(2)}) copy-start(bf16[128,768]{1,0:T(8,128)(2,1)} %param.6) | copy-start | bytes 589828
  28.5 565.5 %all-reduce.16.cloned.1.call-start = ((), (), s32[]{:S(2)}) async-start(), calls=%async_computation.1 | async-start | bytes 7077888 | tf_op jit(solution)/shard_map/psum | solution.py:89
  71.3 0.6 copy-start.55
  301.7 0.6 copy-start.52
  301.7 0.6 copy-start.53
  302.3 0.6 copy-start.50
  310.3 2.7 copy-start.28
  312.9 2.2 copy-start.10
  313.0 2.2 copy-start.12
  314.0 3.9 copy-start.34
  314.0 1.1 copy-start.33
  315.1 2.8 copy-start.36
  316.2 0.9 copy-start.38
  328.4 560.8 %all-reduce.18.cloned.1.call-start = ((), (), s32[]{:S(2)}) async-start(), calls=%async_computation.2 | async-start | bytes 7077888
  339.0 2.9 copy-start.11
  339.0 2.9 copy-start.35
  339.0 2.9 copy-start.37
  339.0 3.0 copy-start.39
  594.0 4.5 copy-start.1
  594.0 4.5 copy-start.2
  594.0 4.5 copy-start.49
  594.0 4.5 copy-start.51
  600.3 1.8 copy-start
  607.6 0.9 copy-start.9
  607.6 2.0 copy-start.46
  608.2 4.0 copy-start.31
  608.2 5.1 copy-start.29
  608.2 1.8 copy-start.41
  608.2 2.3 copy-start.44
  610.5 1.6 copy-start.23
  612.2 1.1 copy-start.14
  612.2 1.3 copy-start.26
  613.3 3.5 copy-start.20
  615.4 0.9 copy-start.18
  615.4 1.4 copy-start.16
  623.4 1.3 copy-start.7
  623.4 1.5 copy-start.19
  623.4 2.2 copy-start.42
  624.9 1.2 copy-start.27
  624.9 1.6 copy-start.32
  624.9 1.6 copy-start.58
  626.5 1.3 copy-start.5
  626.5 1.5 copy-start.17
  628.0 1.6 copy-start.4
  628.0 1.6 copy-start.21
  629.6 1.0 copy-start.15
  629.6 1.3 copy-start.24
  629.6 1.6 copy-start.30
  631.2 1.7 copy-start.54
  631.2 2.5 copy-start.56
Sparse Core Ops, SparseCore 0:
  28.6 269.0 all-reduce.13
  328.5 265.4 all-reduce.15
  623.6 265.5 all-reduce.17
where the time goes:
time: 907 us; the launch traced here: 898 us
  waiting for transfers between devices  728 us (80%)
  local copies, waits for them, and re-layouts  56.6 us (6%)
  blocking collectives  40.9 us (5%)
  matrix products  29.3 us (3%)
  other arithmetic  17.4 us (2%)
  between operations  14.8 us (2%)
  starting transfers between devices  10.7 us (1%)
    unnamed x4, waiting for transfers between devices  255 us
    psum x1, waiting for transfers between devices, on_device(): d_new = lax.psum(flat_new, VIEW_PATCH)  249 us
    psum x1, waiting for transfers between devices, on_device(): summed = lax.psum(flat_terms, VIEW_PATCH)  225 us
    psum x5, blocking collectives, by_axis(): array = lax.psum(array, axis)  40.9 us
  transfers between devices with their start and end apart: 3, of which 3 were waited for; matrix products, arithmetic and copies ran while one was open for 2% of the time, Pallas kernels for 0%

commit v1 on v0

v1 whole, which is shorter than its diff:
```python
import itertools
import math

import jax
import jax.numpy as jnp
from jax import lax
from jax.experimental import pallas as pl
from jax.experimental.pallas import tpu as pltpu
from jax.sharding import PartitionSpec as P

MESH = pl.DeviceIdType.MESH
f32, bf16 = jnp.float32, jnp.bfloat16

step_size = 0.2
epsilon = 1e-06

NX, NY, NZ = 4, 4, 8
HEADS, HD, FF = 4, 192, 384
HALF = FF // 2
ROWS = 128
SLOTS = 8
ALL_ROWS = SLOTS * ROWS
CHUNK = 256
TOTAL_ROWS = ROWS * NX * NY * NZ * 2
COEFFICIENT = step_size * math.sqrt(TOTAL_ROWS)
N_SEMS = 160
GROUP = 6


def device(x, y, z, core):
    return ((x // 2) * 2 + core, (y * 2 + x % 2) * 8 + z)


PARTS = (("x", (0, 1, 2)), ("z", (3, 4)))


def part_sizes(part):
    axis, lane_tiles = part
    first, second = (NX, NZ) if axis == "x" else (NZ, NX)
    row_tiles = HALF // 8 // first
    shard = row_tiles * len(lane_tiles)
    window = -(-shard // second)
    if (shard - window) // (second - 1) >= window:
        window += 1
    return first, second, row_tiles, shard, window


def nt(a, b):
    return lax.dot_general(a, b, (((1,), (1,)), ((), ())), preferred_element_type=f32)


def nn(a, b):
    return lax.dot_general(a, b, (((1,), (0,)), ((), ())), preferred_element_type=f32)


def tn(a, b):
    return lax.dot_general(a, b, (((0,), (0,)), ((), ())), preferred_element_type=f32)


def split(value):
    high = value.astype(bf16)
    return high, (value - high.astype(f32)).astype(bf16)


def tn2(a, b):
    high, low = split(a)
    return tn(high, b) + tn(low, b)


def kernel(
    q_ref, k_ref, v_ref, r_ref, g_ref, w_hbm,
    qg_out, kg_out, vg_out, rg_out, fg_out,
    w_load, w_own, wh, wl, nh, nl, moved, gm, norms,
    kv_send, qg_send, kv, qg, rates,
    kb, vb, qb, gb, ga_s, up_s, t_s,
    s1h, s1l, s2h, s2l, s3h, s3l, s4h, s4l, s5h, s5l, s6h, s6l,
    acc, rate_rows, dq, xq, oq, rq, dkv, xkv, okv, rkv,
    p0_t, p0_r1, p0_s1, p0_r2, p0_s2, p0_a1, p0_f1, p0_g,
    p1_t, p1_r1, p1_s1, p1_r2, p1_s2, p1_a1, p1_f1, p1_g,
    f_t, f_r1, f_s1, f_r2, d_grp, f_msg,
    send_sems, recv_sems, far_sems, load_sems,
):
    view, patch = lax.axis_index("view"), lax.axis_index("patch")
    x, core = (view // 2) * 2 + (patch // 8) % 2, view % 2
    y, z = patch // 16, patch % 8
    mine = view * 64 + patch
    half_block = 2 * y + core

    def peer(axis, offset):
        if axis == "x":
            return device((x + offset) % NX, y, z, core)
        if axis == "y":
            return device(x, (y + offset) % NY, z, core)
        if axis == "z":
            return device(x, y, (z + offset) % NZ, core)
        return device(x, y, z, 1 - core)

    place = {"x": x, "z": z}
    size = {"x": NX, "z": NZ}

    far_group = [32 * (8 * m + half_block) + 8 * x + z for m in range(3)]
    far_owner = [group // 3 for group in far_group]
    near_source = []
    for t in range(3):
        group = 3 * mine + t
        block, rest = group // 32, group % 32
        near_source.append((rest // 8, (block % 8) // 2, rest % 8, block % 2))
    near_index = []
    for sx, sy, sz, sc in near_source:
        sv, sp = device(sx, sy, sz, sc)
        near_index.append(sv * 64 + sp)

    barrier = pltpu.get_barrier_semaphore()
    peers = [("x", d) for d in range(1, NX)] + [("z", d) for d in range(1, NZ)]
    peers += [("y", d) for d in range(1, NY)] + [("core", 1)]
    for axis, offset in peers:
        pl.semaphore_signal(barrier, inc=1, device_id=peer(axis, offset), device_id_type=MESH)
    for t in range(3):
        @pl.when(near_index[t] != mine)
        def _():
            pl.semaphore_signal(barrier, inc=1, device_id=device(*near_source[t]), device_id_type=MESH)

    ids = itertools.count()
    started = []

    def send(src, dst, target):
        which = next(ids)
        copy = pltpu.make_async_remote_copy(
            src_ref=src, dst_ref=dst, send_sem=send_sems.at[which], recv_sem=recv_sems.at[which],
            device_id=target, device_id_type=MESH,
        )
        copy.start()
        started.append(copy)
        return copy

    loads = []
    for m in range(3):
        first = pl.multiple_of(m * HEADS * FF + y * FF, 128)
        load = pltpu.make_async_copy(w_hbm.at[:, pl.ds(first, FF)], w_load.at[m], load_sems.at[m])
        load.start()
        loads.append(load)

    def pack(buffer, left, right):
        for h in range(HEADS):
            cols = slice(HD * h, HD * (h + 1))
            buffer[h, 0:ROWS, 0:HD] = left[:, cols].astype(f32)
            buffer[h, 0:ROWS, HD:2 * HD] = right[:, cols].astype(f32)

    pack(kv_send, k_ref, v_ref)
    for h in range(HEADS):
        kv_send[h, ROWS:ROWS + 8, :] = jnp.zeros((8, 2 * HD), f32)
        kv_send[h, ROWS:ROWS + 8, 0:ROWS] = jnp.broadcast_to(r_ref[h:h + 1, :], (8, ROWS))

    far_count = sum((owner != mine).astype(jnp.int32) for owner in far_owner)
    pl.semaphore_wait(barrier, len(peers) + far_count)

    def scatter_heads(buffer, landing):
        out = {}
        for d in (1, 3, 2):
            out[d] = send(buffer.at[(y + d) % NY], landing.at[d], peer("y", d))
        out["own"] = send(buffer.at[y], landing.at[4], peer("core", 1))
        return out

    def forward(copies, landing):
        passed = []
        for d in (1, 3, 2):
            copies[d].wait_recv()
            passed.append(send(landing.at[d], landing.at[4 + d], peer("core", 1)))
        return passed

    kv_copies = scatter_heads(kv_send, kv)
    pack(qg_send, q_ref, g_ref)
    qg_copies = scatter_heads(qg_send, qg)

    for m in range(3):
        loads[m].wait()
        both = w_load[m]
        own = jnp.where(core == 0, both[:, 0:HALF], both[:, HALF:FF]).T
        w_own[m] = own
        wh[m], wl[m] = split(own)

    def unpack_kv(s):
        kb[s * ROWS:(s + 1) * ROWS, :] = kv[s, 0:ROWS, 0:HD].astype(bf16)
        vb[s * ROWS:(s + 1) * ROWS, :] = kv[s, 0:ROWS, HD:2 * HD].astype(bf16)
        column = kv[s, ROWS:ROWS + 8, 0:ROWS].T
        rates[s * ROWS:(s + 1) * ROWS, :] = column[:, 0:1]

    def unpack_qg(s):
        qb[s * ROWS:(s + 1) * ROWS, :] = qg[s, 0:ROWS, 0:HD].astype(bf16)
        gb[s * ROWS:(s + 1) * ROWS, :] = qg[s, 0:ROWS, HD:2 * HD].astype(bf16)

    kv[0] = kv_send[y]
    qg[0] = qg_send[y]
    passed = forward(kv_copies, kv)
    for s in range(4):
        unpack_kv(s)
    kv_copies["own"].wait_recv()
    for copy in passed:
        copy.wait_recv()
    for s in range(4, 8):
        unpack_kv(s)

    rate_sum = sum(kv[s, ROWS:ROWS + 8, 0:ROWS] for s in range(SLOTS))
    total_part = jnp.sum(rate_sum[0:1, :], axis=1, keepdims=True)

    def silu_parts(gate):
        sig = 1.0 / (1.0 + jnp.exp(-gate))
        act = gate * sig
        slope = sig + act * (1.0 - sig)
        return sig, act, slope

    for m in range(3):
        acc[m] = jnp.zeros((HALF, HD), f32)

    def update_chunk(i, _):
        rows = pl.ds(pl.multiple_of(i * CHUNK, CHUNK), CHUNK)
        keys, values, eta = kb[rows, :], vb[rows, :], rates[rows, :]
        gate = nt(keys, wh[0]) + nt(keys, wl[0])
        up = nt(keys, wh[1]) + nt(keys, wl[1])
        pulled = nt(values, wh[2]) + nt(values, wl[2])
        ga_s[rows, :], up_s[rows, :], t_s[rows, :] = gate, up, pulled
        _, act, slope = silu_parts(gate)
        scaled = eta * pulled
        acc[0] -= tn2(scaled * up * slope, keys)
        acc[1] -= tn2(scaled * act, keys)
        acc[2] -= tn2(eta * act * up, values)
        return 0

    lax.fori_loop(0, ALL_ROWS // CHUNK, update_chunk, 0)

    parts = (
        (p0_t, p0_r1, p0_s1, p0_r2, p0_s2, p0_a1, p0_f1, p0_g),
        (p1_t, p1_r1, p1_s1, p1_r2, p1_s2, p1_a1, p1_f1, p1_g),
    )

    def lanes_of(first, second, third, tail):
        return (
            first[:, 0:128],
            jnp.concatenate([first[:, 128:192], second[:, 0:64]], axis=1),
            second[:, 64:192],
            third[:, 0:128],
            jnp.concatenate([third[:, 128:192], tail], axis=1),
        )

    def start_stage(r, p, source):
        axis, lane_tiles = PARTS[p]
        first, second, row_tiles, shard, window = part_sizes(PARTS[p])
        t = parts[p][0]
        for s in range(first):
            for jj, j in enumerate(lane_tiles):
                block = source[j][s * row_tiles * 8:(s + 1) * row_tiles * 8, :]
                t[r, s * shard + jj * row_tiles:s * shard + (jj + 1) * row_tiles] = block.reshape(row_tiles, 8, 128)
        copies = []
        for d in range(1, first):
            there = (place[axis] + d) % first
            copies.append(send(t.at[r, pl.ds(there * shard, shard)], parts[p][1].at[r, d - 1], peer(axis, d)))
        return copies

    def start_of(p, k):
        _, second, _, shard, window = part_sizes(PARTS[p])
        return ((shard - window) * k) // (second - 1)

    def second_stage(r, p, copies):
        axis = PARTS[p][0]
        other = "z" if axis == "x" else "x"
        first, second, row_tiles, shard, window = part_sizes(PARTS[p])
        t, r1, s1, r2 = parts[p][:4]
        total = t[r, pl.ds(place[axis] * shard, shard)]
        for d in range(1, first):
            copies[d - 1].wait_recv()
            total = total + r1[r, d - 1]
        s1[r] = total
        out = []
        for d in range(1, second):
            there = (place[other] + d) % second
            out.append(send(s1.at[r, pl.ds(start_of(p, there), window)], r2.at[r, d - 1], peer(other, d)))
        return out

    def third_stage(r, p, copies):
        other = "z" if PARTS[p][0] == "x" else "x"
        _, second, _, shard, window = part_sizes(PARTS[p])
        _, _, s1, r2, s2, a1, f1, _ = parts[p]
        total = s1[r, pl.ds(start_of(p, place[other]), window)]
        for d in range(1, second):
            copies[d - 1].wait_recv()
            total = total + r2[r, d - 1]
        s2[r] = total
        return [send(s2.at[r], a1.at[r, d - 1], peer(other, d)) for d in range(1, second)]

    def fourth_stage(r, p, copies):
        axis = PARTS[p][0]
        other = "z" if axis == "x" else "x"
        first, second, _, shard, window = part_sizes(PARTS[p])
        _, _, _, _, s2, a1, f1, g = parts[p]
        f1[r, pl.ds(start_of(p, place[other]), window)] = s2[r]
        for d in range(1, second):
            copies[d - 1].wait_recv()
            there = (place[other] + second - d) % second
            f1[r, pl.ds(start_of(p, there), window)] = a1[r, d - 1]
        here = pl.ds(place[axis] * shard, shard)
        out = [send(f1.at[r], g.at[r, here], peer(axis, d)) for d in range(1, first)]
        g[r, here] = f1[r]
        return out

    def gathered(r, copies):
        for group in copies:
            for copy in group:
                copy.wait_recv()
        tiles = {}
        for p in range(2):
            first, _, row_tiles, shard, _ = part_sizes(PARTS[p])
            for jj, j in enumerate(PARTS[p][1]):
                rows = [
                    parts[p][7][r, s * shard + jj * row_tiles:s * shard + (jj + 1) * row_tiles].reshape(row_tiles * 8, 128)
                    for s in range(first)
                ]
                tiles[j] = jnp.concatenate(rows, axis=0)
        gate = jnp.concatenate([tiles[0], tiles[1][:, 0:64]], axis=1)
        up = jnp.concatenate([tiles[1][:, 64:128], tiles[2]], axis=1)
        down = jnp.concatenate([tiles[3], tiles[4][:, 0:64]], axis=1)
        return gate, up, down, tiles[4][:, 64:128]

    def reduce_all(r, tail, between):
        source = lanes_of(acc[0], acc[1], acc[2], tail)
        copies = [start_stage(r, p, source) for p in range(2)]
        between()
        copies = [second_stage(r, p, copies[p]) for p in range(2)]
        copies = [third_stage(r, p, copies[p]) for p in range(2)]
        copies = [fourth_stage(r, p, copies[p]) for p in range(2)]
        return gathered(r, copies)

    def take_queries():
        passed = forward(qg_copies, qg)
        for s in range(4):
            unpack_qg(s)
        qg_copies["own"].wait_recv()
        for copy in passed:
            copy.wait_recv()
        for s in range(4, 8):
            unpack_qg(s)

    *terms, tail = reduce_all(0, jnp.broadcast_to(total_part, (HALF, 64)), take_queries)
    totals = tail[0:1, 0:1]
    scale = COEFFICIENT / totals
    for m in range(3):
        weight = w_own[m]
        change = terms[m] * scale
        shifted = weight - change
        init_norm = jnp.sqrt(jnp.sum(weight * weight, axis=1, keepdims=True) + epsilon)
        inverse = lax.rsqrt(jnp.sum(shifted * shifted, axis=1, keepdims=True) + epsilon)
        gm[m], moved[m] = change, shifted
        norms[m, 0], norms[m, 1] = init_norm, inverse
        nh[m], nl[m] = split(shifted * (init_norm * inverse))
        acc[m] = jnp.zeros((HALF, HD), f32)

    def apply_chunk(i, _):
        rows = pl.ds(pl.multiple_of(i * CHUNK, CHUNK), CHUNK)
        queries, grads = qb[rows, :], gb[rows, :]
        gate = nt(queries, nh[0]) + nt(queries, nl[0])
        up = nt(queries, nh[1]) + nt(queries, nl[1])
        pulled = nt(grads, nh[2]) + nt(grads, nl[2])
        _, act, slope = silu_parts(gate)
        d_gate_h, d_gate_l = split(pulled * up * slope)
        d_up_h, d_up_l = split(pulled * act)
        acc[0] += tn(d_gate_h, queries) + tn(d_gate_l, queries)
        acc[1] += tn(d_up_h, queries) + tn(d_up_l, queries)
        acc[2] += tn2(act * up, grads)
        s1h[rows, :], s1l[rows, :] = d_gate_h, d_gate_l
        s2h[rows, :], s2l[rows, :] = d_up_h, d_up_l
        return 0

    lax.fori_loop(0, ALL_ROWS // CHUNK, apply_chunk, 0)

    def product(ah, al, bh, bl, rows):
        high = ah[rows, :]
        return nn(high, bh) + nn(high, bl) + nn(al[rows, :], bh)

    def query_chunk(i, _):
        rows = pl.ds(pl.multiple_of(i * ROWS, ROWS), ROWS)
        dq[i] = product(s1h, s1l, nh[0], nl[0], rows) + product(s2h, s2l, nh[1], nl[1], rows)
        return 0

    query_copies = {}

    def send_queries():
        lax.fori_loop(0, SLOTS, query_chunk, 0)
        query_copies["pair"] = send(dq.at[pl.ds(4, 4)], xq, peer("core", 1))

    def return_rows(pair, partial, arrived, sums, landing):
        pair.wait_recv()
        out = []
        for d in (1, 3, 2, 0):
            if d == 0:
                landing[0] = partial[0] + arrived[0]
            else:
                sums[d] = partial[d] + arrived[d]
                out.append(send(sums.at[d], landing.at[d], peer("y", NY - d)))
        return out

    d_new = reduce_all(1, jnp.zeros((HALF, 64), f32), send_queries)
    query_back = return_rows(query_copies["pair"], dq, xq, oq, rq)

    head_part = jnp.zeros((1, 1), f32)
    direct = []
    for m in range(3):
        init_norm, inverse = norms[m, 0], norms[m, 1]
        weight, shifted = w_own[m], moved[m]
        dots = jnp.sum(d_new[m] * shifted, axis=1, keepdims=True)
        d_moved = d_new[m] * (init_norm * inverse) - shifted * (dots * init_norm * inverse * inverse * inverse)
        direct.append(d_moved + weight * (dots * inverse / init_norm))
        by_row = jnp.sum(d_moved * gm[m], axis=1, keepdims=True)
        head_part = head_part - jnp.sum(by_row, axis=0, keepdims=True)
        nh[m], nl[m] = split(d_moved * scale)
        acc[m] = jnp.zeros((HALF, HD), f32)
    d_totals = -head_part / totals
    direct_tiles = lanes_of(*direct, jnp.zeros((HALF, 64), f32))
    for j in range(5):
        for n in range(HALF // GROUP):
            d_grp[n, 0:GROUP, 128 * j:128 * (j + 1)] = direct_tiles[j][GROUP * n:GROUP * (n + 1), :]

    def pull_chunk(i, _):
        rows = pl.ds(pl.multiple_of(i * CHUNK, CHUNK), CHUNK)
        keys, values, eta = kb[rows, :], vb[rows, :], rates[rows, :]
        gate, up, pulled = ga_s[rows, :], up_s[rows, :], t_s[rows, :]
        one = nt(keys, nh[0]) + nt(keys, nl[0])
        two = nt(keys, nh[1]) + nt(keys, nl[1])
        three = nt(values, nh[2]) + nt(values, nl[2])
        sig, act, slope = silu_parts(gate)
        curve = sig * (1.0 - sig) * (2.0 + gate * (1.0 - 2.0 * sig))
        up_slope = up * slope
        mix = one * up_slope + two * act
        hidden = act * up
        by_rate_h, by_rate_l = split(mix * pulled + three * hidden)
        ones = jnp.ones((8, HALF), bf16)
        rate_rows[i] = nt(ones, by_rate_h) + nt(ones, by_rate_l)
        scaled = eta * pulled
        eta_three = eta * three
        c_gate_h, c_gate_l = split(scaled * (one * up * curve + two * slope) + eta_three * up_slope)
        c_up_h, c_up_l = split(scaled * one * slope + eta_three * act)
        c_pull_h, c_pull_l = split(eta * mix)
        acc[0] += tn(c_gate_h, keys) + tn(c_gate_l, keys)
        acc[1] += tn(c_up_h, keys) + tn(c_up_l, keys)
        acc[2] += tn(c_pull_h, values) + tn(c_pull_l, values)
        s1h[rows, :], s1l[rows, :] = c_gate_h, c_gate_l
        s2h[rows, :], s2l[rows, :] = c_up_h, c_up_l
        s3h[rows, :], s3l[rows, :] = c_pull_h, c_pull_l
        s4h[rows, :], s4l[rows, :] = split(scaled * up_slope)
        s5h[rows, :], s5l[rows, :] = split(scaled * act)
        s6h[rows, :], s6l[rows, :] = split(eta * hidden)
        return 0

    lax.fori_loop(0, ALL_ROWS // CHUNK, pull_chunk, 0)

    tiles = lanes_of(acc[0], acc[1], acc[2], jnp.zeros((HALF, 64), f32))
    for j in range(5):
        f_t[:, 128 * j:128 * (j + 1)] = tiles[j]
    x_rows = HALF // NX
    weight_copies = []
    for d in range(1, NX):
        first = pl.multiple_of(((x + d) % NX) * x_rows, x_rows)
        weight_copies.append(send(f_t.at[pl.ds(first, x_rows)], f_r1.at[d - 1], peer("x", d)))

    def key_chunk(i, _):
        rows = pl.ds(pl.multiple_of(i * ROWS, ROWS), ROWS)
        key_part = product(s1h, s1l, wh[0], wl[0], rows) + product(s2h, s2l, wh[1], wl[1], rows)
        key_part += product(s4h, s4l, nh[0], nl[0], rows) + product(s5h, s5l, nh[1], nl[1], rows)
        value_part = product(s3h, s3l, wh[2], wl[2], rows) + product(s6h, s6l, nh[2], nl[2], rows)
        dkv[i, 0:ROWS, 0:HD] = key_part
        dkv[i, 0:ROWS, HD:2 * HD] = value_part
        return 0

    lax.fori_loop(0, SLOTS, key_chunk, 0)
    for s in range(SLOTS):
        dkv[s, ROWS:ROWS + 8, :] = jnp.zeros((8, 2 * HD), f32)
        lane = (s % 2) * ROWS
        dkv[s, ROWS:ROWS + 8, 0:ROWS] = rate_rows[s // 2, :, lane:lane + ROWS] + d_totals
    pair = send(dkv.at[pl.ds(4, 4)], xkv, peer("core", 1))

    total = f_t[pl.ds(pl.multiple_of(x * x_rows, x_rows), x_rows), :]
    for d in range(1, NX):
        weight_copies[d - 1].wait_recv()
        total = total + f_r1[d - 1]
    for n in range(NZ):
        f_s1[n, 0:GROUP, :] = total[GROUP * n:GROUP * (n + 1), :]
        f_s1[n, GROUP:8, :] = jnp.zeros((8 - GROUP, 640), f32)
    weight_copies = [send(f_s1.at[(z + d) % NZ], f_r2.at[d - 1], peer("z", d)) for d in range(1, NZ)]
    row_back = return_rows(pair, dkv, xkv, okv, rkv)

    total = f_s1[z]
    for d in range(1, NZ):
        weight_copies[d - 1].wait_recv()
        total = total + f_r2[d - 1]
    total = (total + d_grp[8 * x + z]) * (1.0 / math.sqrt(TOTAL_ROWS))
    f_msg[0, :, 0:HD] = total[:, 0:HD]
    f_msg[1, :, 0:HD] = total[:, HD:2 * HD]
    f_msg[2, :, 0:HD] = total[:, 2 * HD:3 * HD]
    far_copies = []
    for m in range(3):
        slot = far_group[m] % 3
        owner = far_owner[m]
        copy = pltpu.make_async_remote_copy(
            src_ref=f_msg.at[m], dst_ref=fg_out.at[slot], send_sem=far_sems.at[0, m], recv_sem=far_sems.at[1, slot],
            device_id=(owner // 64, owner % 64), device_id_type=MESH,
        )

        @pl.when(owner != mine)
        def _():
            copy.start()

        @pl.when(owner == mine)
        def _():
            fg_out[slot] = f_msg[m]

        far_copies.append(copy)

    def rows_out(out_ref, landing, lanes):
        for h in range(HEADS):
            d = (h + NY - y) % NY
            out_ref[:, HD * h:HD * (h + 1)] = landing[d, 0:ROWS, lanes:lanes + HD].astype(bf16)

    for copy in query_back:
        copy.wait_recv()
    rows_out(qg_out, rq, 0)
    for copy in row_back:
        copy.wait_recv()
    rows_out(kg_out, rkv, 0)
    rows_out(vg_out, rkv, HD)
    for h in range(HEADS):
        rg_out[h] = rkv[(h + NY - y) % NY, ROWS:ROWS + 8, 0:ROWS]

    for m in range(3):
        @pl.when(near_index[m] != mine)
        def _():
            pltpu.make_async_remote_copy(
                src_ref=f_msg.at[m], dst_ref=fg_out.at[m], send_sem=far_sems.at[0, m], recv_sem=far_sems.at[1, m],
                device_id=(view, patch), device_id_type=MESH,
            ).wait_recv()

        @pl.when(far_owner[m] != mine)
        def _():
            far_copies[m].wait_send()
    for copy in started:
        copy.wait_send()


def scratch():
    tile = (8, 128)
    shapes = [
        pltpu.VMEM((3, HD, FF), f32),
        pltpu.VMEM((3, HALF, HD), f32),
        *[pltpu.VMEM((3, HALF, HD), bf16)] * 4,
        *[pltpu.VMEM((3, HALF, HD), f32)] * 2,
        pltpu.VMEM((3, 2, HALF, 1), f32),
        *[pltpu.VMEM((HEADS, ROWS + 8, 2 * HD), f32)] * 2,
        *[pltpu.VMEM((SLOTS, ROWS + 8, 2 * HD), f32)] * 2,
        pltpu.VMEM((ALL_ROWS, 1), f32),
        *[pltpu.VMEM((ALL_ROWS, HD), bf16)] * 4,
        *[pltpu.VMEM((ALL_ROWS, HALF), f32)] * 3,
        *[pltpu.VMEM((ALL_ROWS, HALF), bf16)] * 12,
        pltpu.VMEM((3, HALF, HD), f32),
        pltpu.VMEM((ALL_ROWS // CHUNK, 8, CHUNK), f32),
        pltpu.VMEM((SLOTS, ROWS, HD), f32),
        *[pltpu.VMEM((4, ROWS, HD), f32)] * 3,
        pltpu.VMEM((SLOTS, ROWS + 8, 2 * HD), f32),
        *[pltpu.VMEM((4, ROWS + 8, 2 * HD), f32)] * 3,
    ]
    for part in PARTS:
        first, second, _, shard, window = part_sizes(part)
        shapes += [
            pltpu.VMEM((2, first * shard) + tile, f32),
            pltpu.VMEM((2, first - 1, shard) + tile, f32),
            pltpu.VMEM((2, shard) + tile, f32),
            pltpu.VMEM((2, second - 1, window) + tile, f32),
            pltpu.VMEM((2, window) + tile, f32),
            pltpu.VMEM((2, second - 1, window) + tile, f32),
            pltpu.VMEM((2, shard) + tile, f32),
            pltpu.VMEM((2, first * shard) + tile, f32),
        ]
    shapes += [
        pltpu.VMEM((HALF, 640), f32),
        pltpu.VMEM((NX - 1, HALF // NX, 640), f32),
        pltpu.VMEM((NZ, 8, 640), f32),
        pltpu.VMEM((NZ - 1, 8, 640), f32),
        pltpu.VMEM((HALF // GROUP, 8, 640), f32),
        pltpu.VMEM((3, 8, 256), f32),
        pltpu.SemaphoreType.DMA((N_SEMS,)),
        pltpu.SemaphoreType.DMA((N_SEMS,)),
        pltpu.SemaphoreType.DMA((2, 3)),
        pltpu.SemaphoreType.DMA((3,)),
    ]
    return shapes


def on_device(queries, key_rows, value_rows, step_rates, fast_init, out_grad):
    vmem = pl.BlockSpec(memory_space=pltpu.VMEM)
    rows = jax.ShapeDtypeStruct((ROWS, HEADS * HD), bf16)
    query_grad, key_grad, value_grad, rate_tiles, groups = pl.pallas_call(
        kernel,
        out_shape=(
            rows, rows, rows,
            jax.ShapeDtypeStruct((HEADS, 8, ROWS), f32),
            jax.ShapeDtypeStruct((3, 8, 256), f32),
        ),
        in_specs=[vmem] * 5 + [pl.BlockSpec(memory_space=pl.ANY)],
        out_specs=(vmem,) * 5,
        scratch_shapes=scratch(),
        compiler_params=pltpu.CompilerParams(
            collective_id=0, has_side_effects=True, vmem_limit_bytes=56 * 2**20
        ),
        name="layer_grad",
    )(queries, key_rows, value_rows, step_rates.T, out_grad, fast_init)
    rate_grad = rate_tiles[:, 0, :].T
    fast_grad = groups[:, :GROUP, :HD].reshape(3 * GROUP, HD).T
    return query_grad, key_grad, value_grad, rate_grad, fast_grad


def solution(mesh):
    both = ("view", "patch")
    return jax.shard_map(
        on_device,
        mesh=mesh,
        in_specs=(P(both, None), P(both, None), P(both, None), P(both, None), P(), P(both, None)),
        out_specs=(P(both, None), P(both, None), P(both, None), P(both, None), P(None, both)),
        check_vma=False,
    )
```

time: 907 us -> 117 us (0.13)
  waiting for transfers between devices: 728 us -> 0 us
  Pallas kernels: 0 us -> 107 us
  local copies, waits for them, and re-layouts: 56.6 us -> 7.49 us
  blocking collectives: 40.9 us -> 0 us
  matrix products: 29.3 us -> 0 us
  other arithmetic: 17.4 us -> 0 us
  between operations: 14.8 us -> 0.64 us
  starting transfers between devices: 10.7 us -> 0 us
    psum x2 -> x0, waiting for transfers between devices: 474 us -> none  [the longest x1 249 us: on_device(): d_new = lax.psum(flat_new, VIEW_PATCH)]
    unnamed x4 -> x0, waiting for transfers between devices: 255 us -> none
    pallas_call x0 -> x1, Pallas kernels: none -> 107 us  [on_device(): pl.pallas_call(kernel, out_shape=(rows, rows, rows, jax.ShapeDtypeStruct(...]
    psum x5 -> x0, blocking collectives: 40.9 us -> none  [by_axis(): array = lax.psum(array, axis)]
    dot_general x28 -> x0, matrix products: 29.3 us -> none  [the longest x9 10.9 us: fast_apply(): jnp.einsum('rhd,dhc->rhc', inputs, weights[:, 1], precision=product_preci...]
    reshape x7 -> x1, local copies, waits for them, and re-layouts: 24.8 us -> 1.35 us  [on_device(): fast_grad = groups[:, :GROUP, :HD].reshape(3 * GROUP, HD).T]
    unnamed x125 -> x3, local copies, waits for them, and re-layouts: 17.1 us -> 4.85 us
    unnamed x1 -> x0, starting transfers between devices: 10.6 us -> none
  transfers between devices with their start and end apart: 3 -> 0, of which waited for: 3 -> 0; matrix products, arithmetic and copies ran while one was open for 2% -> 0% of each run, Pallas kernels for 0% -> 0%
where the time goes in v1:
time: 117 us; the launch traced here: 115 us
  Pallas kernels  107 us (91%)
  local copies, waits for them, and re-layouts  7.49 us (6%)
    pallas_call x1, Pallas kernels, on_device(): pl.pallas_call(kernel, out_shape=(rows, rows, rows, jax.ShapeDtypeStruct(...  107 us
    unnamed x3, local copies, waits for them, and re-layouts  4.85 us

profile of v1, /device:TPU:1, one launch (start us, length us, event | category | flops | bytes accessed | tf_op | source)
XLA Modules:
  0.0 115.0 jit_solution(437683805917552569)
XLA Ops:
  0.6 106.9 %layer_grad.1 = (bf16[128,768]{1,0:T(8,128)(2,1)}, bf16[128,768]{1,0:T(8,128)(2,1)}, bf16[128,768]{1,0:T(8,128)(2,1)}, f32[4,8,128]{2,1,0:T(8,128)}, f32[3,8,256]{2,1,0:T(8,128)}) custom-call(bf16[128,768]{1,0:T(8,128)(2,1)} %q_ref.1, bf16[128,768]{1,0:T(8,128)(2,1)} %k_ref.1, bf16[128,768]{1,0:T(8,128)(2,1)} %v_ref.1, f32[4,128]{1,0:T(4,128)} %bitcast.8, ...), custom_call_target="tpu_custom_call" | custom-call | tf_op jit(solution)/shard_map/layer_grad/pallas_call | solution.py:597
  107.5 1.3 %slice.6 = f32[4,1,128]{2,1,0:T(1,128)} slice(f32[4,8,128]{2,1,0:T(8,128)} %get-tuple-element.13), slice={[0:4], [0:1], [0:128]} | slice | bytes 4096 | tf_op jit(solution)/shard_map/slice | solution.py:612
  108.8 1.3 %reshape.13 = f32[18,192]{1,0:T(8,128)} reshape(f32[3,6,192]{2,1,0:T(8,128)} %bitcast.7) | data formatting | bytes 27648 | tf_op jit(solution)/shard_map/reshape | solution.py:613
  110.2 1.6 %copy.14 = bf16[128,768]{1,0:T(8,128)(2,1)} copy(bf16[128,768]{1,0:T(8,128)(2,1)} %get-tuple-element.20) | data formatting | bytes 393216
  111.8 1.6 %copy.15 = bf16[128,768]{1,0:T(8,128)(2,1)} copy(bf16[128,768]{1,0:T(8,128)(2,1)} %get-tuple-element.21) | data formatting | bytes 393216
  113.4 1.6 %copy.16 = bf16[128,768]{1,0:T(8,128)(2,1)} copy(bf16[128,768]{1,0:T(8,128)(2,1)} %get-tuple-element.22) | data formatting | bytes 393216

commit v2 on v1

--- a/solution.py
+++ b/solution.py
@@ -69,10 +69,10 @@
 
 def kernel(
     q_ref, k_ref, v_ref, r_ref, g_ref, w_hbm,
-    qg_out, kg_out, vg_out, rg_out, fg_out,
+    rows_ref, rg_out, fg_out,
     w_load, w_own, wh, wl, nh, nl, moved, gm, norms,
     kv_send, qg_send, kv, qg, rates,
-    kb, vb, qb, gb, ga_s, up_s, t_s,
+    inv_rates, kb, vb, qb, gb, ga_s, up_s, t_s, m1, m2, m3, m4,
     s1h, s1l, s2h, s2l, s3h, s3l, s4h, s4l, s5h, s5l, s6h, s6l,
     acc, rate_rows, dq, xq, oq, rq, dkv, xkv, okv, rkv,
     p0_t, p0_r1, p0_s1, p0_r2, p0_s2, p0_a1, p0_f1, p0_g,
@@ -161,16 +161,8 @@
         out["own"] = send(buffer.at[y], landing.at[4], peer("core", 1))
         return out
 
-    def forward(copies, landing):
-        passed = []
-        for d in (1, 3, 2):
-            copies[d].wait_recv()
-            passed.append(send(landing.at[d], landing.at[4 + d], peer("core", 1)))
-        return passed
-
     kv_copies = scatter_heads(kv_send, kv)
     pack(qg_send, q_ref, g_ref)
-    qg_copies = scatter_heads(qg_send, qg)
 
     for m in range(3):
         loads[m].wait()
@@ -179,29 +171,20 @@
         w_own[m] = own
         wh[m], wl[m] = split(own)
 
+    def row_block(s):
+        first = (s % 4) * CHUNK + (s // 4) * ROWS
+        return slice(first, first + ROWS)
+
     def unpack_kv(s):
-        kb[s * ROWS:(s + 1) * ROWS, :] = kv[s, 0:ROWS, 0:HD].astype(bf16)
-        vb[s * ROWS:(s + 1) * ROWS, :] = kv[s, 0:ROWS, HD:2 * HD].astype(bf16)
-        column = kv[s, ROWS:ROWS + 8, 0:ROWS].T
-        rates[s * ROWS:(s + 1) * ROWS, :] = column[:, 0:1]
+        kb[row_block(s), :] = kv[s, 0:ROWS, 0:HD].astype(bf16)
+        vb[row_block(s), :] = kv[s, 0:ROWS, HD:2 * HD].astype(bf16)
+        column = kv[s, ROWS:ROWS + 8, 0:ROWS].T[:, 0:1]
+        rates[row_block(s), :] = column
+        inv_rates[row_block(s), :] = 1.0 / column
 
     def unpack_qg(s):
-        qb[s * ROWS:(s + 1) * ROWS, :] = qg[s, 0:ROWS, 0:HD].astype(bf16)
-        gb[s * ROWS:(s + 1) * ROWS, :] = qg[s, 0:ROWS, HD:2 * HD].astype(bf16)
-
-    kv[0] = kv_send[y]
-    qg[0] = qg_send[y]
-    passed = forward(kv_copies, kv)
-    for s in range(4):
-        unpack_kv(s)
-    kv_copies["own"].wait_recv()
-    for copy in passed:
-        copy.wait_recv()
-    for s in range(4, 8):
-        unpack_kv(s)
-
-    rate_sum = sum(kv[s, ROWS:ROWS + 8, 0:ROWS] for s in range(SLOTS))
-    total_part = jnp.sum(rate_sum[0:1, :], axis=1, keepdims=True)
+        qb[row_block(s), :] = qg[s, 0:ROWS, 0:HD].astype(bf16)
+        gb[row_block(s), :] = qg[s, 0:ROWS, HD:2 * HD].astype(bf16)
 
     def silu_parts(gate):
         sig = 1.0 / (1.0 + jnp.exp(-gate))
@@ -212,8 +195,8 @@
     for m in range(3):
         acc[m] = jnp.zeros((HALF, HD), f32)
 
-    def update_chunk(i, _):
-        rows = pl.ds(pl.multiple_of(i * CHUNK, CHUNK), CHUNK)
+    def update_chunk(i):
+        rows = slice(i * CHUNK, (i + 1) * CHUNK)
         keys, values, eta = kb[rows, :], vb[rows, :], rates[rows, :]
         gate = nt(keys, wh[0]) + nt(keys, wl[0])
         up = nt(keys, wh[1]) + nt(keys, wl[1])
@@ -224,9 +207,37 @@
         acc[0] -= tn2(scaled * up * slope, keys)
         acc[1] -= tn2(scaled * act, keys)
         acc[2] -= tn2(eta * act * up, values)
-        return 0
-
-    lax.fori_loop(0, ALL_ROWS // CHUNK, update_chunk, 0)
+
+    def take_pair(d):
+        unpack_kv(d)
+        unpack_kv(4 + d)
+        update_chunk(d)
+
+    def pass_on(copies, landing, d):
+        copies[d].wait_recv()
+        return send(landing.at[d], landing.at[4 + d], peer("core", 1))
+
+    with jax.named_scope("keys_own"):
+        kv[0] = kv_send[y]
+        kv_copies["own"].wait_recv()
+        take_pair(0)
+    passed = {}
+    with jax.named_scope("keys_first"):
+        passed[1] = pass_on(kv_copies, kv, 1)
+        passed[3] = pass_on(kv_copies, kv, 3)
+        passed[1].wait_recv()
+        take_pair(1)
+    with jax.named_scope("keys_second"):
+        passed[2] = pass_on(kv_copies, kv, 2)
+        qg_copies = scatter_heads(qg_send, qg)
+        passed[3].wait_recv()
+        take_pair(3)
+    with jax.named_scope("keys_third"):
+        passed[2].wait_recv()
+        take_pair(2)
+
+    rate_sum = sum(kv[s, ROWS:ROWS + 8, 0:ROWS] for s in range(SLOTS))
+    total_part = jnp.sum(rate_sum[0:1, :], axis=1, keepdims=True)
 
     parts = (
         (p0_t, p0_r1, p0_s1, p0_r2, p0_s2, p0_a1, p0_f1, p0_g),
@@ -320,28 +331,61 @@
         down = jnp.concatenate([tiles[3], tiles[4][:, 0:64]], axis=1)
         return gate, up, down, tiles[4][:, 64:128]
 
-    def reduce_all(r, tail, between):
-        source = lanes_of(acc[0], acc[1], acc[2], tail)
-        copies = [start_stage(r, p, source) for p in range(2)]
-        between()
-        copies = [second_stage(r, p, copies[p]) for p in range(2)]
-        copies = [third_stage(r, p, copies[p]) for p in range(2)]
-        copies = [fourth_stage(r, p, copies[p]) for p in range(2)]
-        return gathered(r, copies)
+    def reduce_all(r, tail, hooks):
+        with jax.named_scope("first_sends"):
+            source = lanes_of(acc[0], acc[1], acc[2], tail)
+            copies = [start_stage(r, p, source) for p in (1, 0)][::-1]
+        with jax.named_scope("first_hook"):
+            hooks[0]()
+        with jax.named_scope("second_sends"):
+            copies = [second_stage(r, p, copies[p]) for p in range(2)]
+        with jax.named_scope("second_hook"):
+            hooks[1]()
+        with jax.named_scope("third_sends"):
+            copies = [third_stage(r, p, copies[p]) for p in range(2)]
+        with jax.named_scope("third_hook"):
+            hooks[2]()
+        with jax.named_scope("fourth_sends"):
+            copies = [fourth_stage(r, p, copies[p]) for p in range(2)]
+        with jax.named_scope("gathered"):
+            return gathered(r, copies)
+
+    def prepare_chunk(i, _):
+        rows = pl.ds(pl.multiple_of(i * CHUNK, CHUNK), CHUNK)
+        eta, gate, up, pulled = rates[rows, :], ga_s[rows, :], up_s[rows, :], t_s[rows, :]
+        sig, act, slope = silu_parts(gate)
+        curve = sig * (1.0 - sig) * (2.0 + gate * (1.0 - 2.0 * sig))
+        scaled = eta * pulled
+        by_slope, by_act = eta * (up * slope), eta * act
+        m1[rows, :], m2[rows, :] = scaled * up * curve, scaled * slope
+        m3[rows, :], m4[rows, :] = by_slope, by_act
+        s4h[rows, :], s4l[rows, :] = split(by_slope * pulled)
+        s5h[rows, :], s5l[rows, :] = split(by_act * pulled)
+        s6h[rows, :], s6l[rows, :] = split(by_act * up)
+        return 0
+
+    query_passed = {}
+
+    def prepare():
+        lax.fori_loop(0, ALL_ROWS // CHUNK, prepare_chunk, 0)
+
+    def pass_queries():
+        qg[0] = qg_send[y]
+        for d in (1, 3, 2):
+            query_passed[d] = pass_on(qg_copies, qg, d)
 
     def take_queries():
-        passed = forward(qg_copies, qg)
-        for s in range(4):
+        qg_copies["own"].wait_recv()
+        for d in (1, 3, 2):
+            query_passed[d].wait_recv()
+        for s in range(SLOTS):
             unpack_qg(s)
-        qg_copies["own"].wait_recv()
-        for copy in passed:
-            copy.wait_recv()
-        for s in range(4, 8):
-            unpack_qg(s)
-
-    *terms, tail = reduce_all(0, jnp.broadcast_to(total_part, (HALF, 64)), take_queries)
+
+    *terms, tail = reduce_all(0, jnp.broadcast_to(total_part, (HALF, 64)), (prepare, pass_queries, take_queries))
     totals = tail[0:1, 0:1]
     scale = COEFFICIENT / totals
+    new_scope = jax.named_scope("new_weights")
+    new_scope.__enter__()
     for m in range(3):
         weight = w_own[m]
         change = terms[m] * scale
@@ -352,6 +396,8 @@
         norms[m, 0], norms[m, 1] = init_norm, inverse
         nh[m], nl[m] = split(shifted * (init_norm * inverse))
         acc[m] = jnp.zeros((HALF, HD), f32)
+
+    new_scope.__exit__(None, None, None)
 
     def apply_chunk(i, _):
         rows = pl.ds(pl.multiple_of(i * CHUNK, CHUNK), CHUNK)
@@ -369,7 +415,8 @@
         s2h[rows, :], s2l[rows, :] = d_up_h, d_up_l
         return 0
 
-    lax.fori_loop(0, ALL_ROWS // CHUNK, apply_chunk, 0)
+    with jax.named_scope("apply"):
+        lax.fori_loop(0, ALL_ROWS // CHUNK, apply_chunk, 0)
 
     def product(ah, al, bh, bl, rows):
         high = ah[rows, :]
@@ -377,7 +424,8 @@
 
     def query_chunk(i, _):
         rows = pl.ds(pl.multiple_of(i * ROWS, ROWS), ROWS)
-        dq[i] = product(s1h, s1l, nh[0], nl[0], rows) + product(s2h, s2l, nh[1], nl[1], rows)
+        slot = (i % 2) * 4 + i // 2
+        dq[slot] = product(s1h, s1l, nh[0], nl[0], rows) + product(s2h, s2l, nh[1], nl[1], rows)
         return 0
 
     query_copies = {}
@@ -397,9 +445,14 @@
                 out.append(send(sums.at[d], landing.at[d], peer("y", NY - d)))
         return out
 
-    d_new = reduce_all(1, jnp.zeros((HALF, 64), f32), send_queries)
-    query_back = return_rows(query_copies["pair"], dq, xq, oq, rq)
-
+    def return_queries():
+        query_copies["back"] = return_rows(query_copies["pair"], dq, xq, oq, rq)
+
+    d_new = reduce_all(1, jnp.zeros((HALF, 64), f32), (send_queries, return_queries, lambda: None))
+    query_back = query_copies["back"]
+
+    pre_scope = jax.named_scope("pull_weights")
+    pre_scope.__enter__()
     head_part = jnp.zeros((1, 1), f32)
     direct = []
     for m in range(3):
@@ -413,43 +466,33 @@
         nh[m], nl[m] = split(d_moved * scale)
         acc[m] = jnp.zeros((HALF, HD), f32)
     d_totals = -head_part / totals
-    direct_tiles = lanes_of(*direct, jnp.zeros((HALF, 64), f32))
-    for j in range(5):
-        for n in range(HALF // GROUP):
-            d_grp[n, 0:GROUP, 128 * j:128 * (j + 1)] = direct_tiles[j][GROUP * n:GROUP * (n + 1), :]
+    pre_scope.__exit__(None, None, None)
 
     def pull_chunk(i, _):
         rows = pl.ds(pl.multiple_of(i * CHUNK, CHUNK), CHUNK)
-        keys, values, eta = kb[rows, :], vb[rows, :], rates[rows, :]
-        gate, up, pulled = ga_s[rows, :], up_s[rows, :], t_s[rows, :]
+        keys, values = kb[rows, :], vb[rows, :]
         one = nt(keys, nh[0]) + nt(keys, nl[0])
         two = nt(keys, nh[1]) + nt(keys, nl[1])
         three = nt(values, nh[2]) + nt(values, nl[2])
-        sig, act, slope = silu_parts(gate)
-        curve = sig * (1.0 - sig) * (2.0 + gate * (1.0 - 2.0 * sig))
-        up_slope = up * slope
-        mix = one * up_slope + two * act
-        hidden = act * up
-        by_rate_h, by_rate_l = split(mix * pulled + three * hidden)
-        ones = jnp.ones((8, HALF), bf16)
-        rate_rows[i] = nt(ones, by_rate_h) + nt(ones, by_rate_l)
-        scaled = eta * pulled
-        eta_three = eta * three
-        c_gate_h, c_gate_l = split(scaled * (one * up * curve + two * slope) + eta_three * up_slope)
-        c_up_h, c_up_l = split(scaled * one * slope + eta_three * act)
-        c_pull_h, c_pull_l = split(eta * mix)
+        by_slope, by_act, by_two = m3[rows, :], m4[rows, :], m2[rows, :]
+        c_pull = one * by_slope + two * by_act
+        c_gate_h, c_gate_l = split(one * m1[rows, :] + two * by_two + three * by_slope)
+        c_up_h, c_up_l = split(one * by_two + three * by_act)
+        c_pull_h, c_pull_l = split(c_pull)
         acc[0] += tn(c_gate_h, keys) + tn(c_gate_l, keys)
         acc[1] += tn(c_up_h, keys) + tn(c_up_l, keys)
         acc[2] += tn(c_pull_h, values) + tn(c_pull_l, values)
+        by_rate = c_pull * t_s[rows, :] + three * (by_act * up_s[rows, :])
+        by_rate_h, by_rate_l = split(by_rate * inv_rates[rows, :])
+        ones = jnp.ones((8, HALF), bf16)
+        rate_rows[i] = nt(ones, by_rate_h) + nt(ones, by_rate_l)
         s1h[rows, :], s1l[rows, :] = c_gate_h, c_gate_l
         s2h[rows, :], s2l[rows, :] = c_up_h, c_up_l
         s3h[rows, :], s3l[rows, :] = c_pull_h, c_pull_l
-        s4h[rows, :], s4l[rows, :] = split(scaled * up_slope)
-        s5h[rows, :], s5l[rows, :] = split(scaled * act)
-        s6h[rows, :], s6l[rows, :] = split(eta * hidden)
         return 0
 
-    lax.fori_loop(0, ALL_ROWS // CHUNK, pull_chunk, 0)
+    with jax.named_scope("pull"):
+        lax.fori_loop(0, ALL_ROWS // CHUNK, pull_chunk, 0)
 
     tiles = lanes_of(acc[0], acc[1], acc[2], jnp.zeros((HALF, 64), f32))
     for j in range(5):
@@ -462,30 +505,41 @@
 
     def key_chunk(i, _):
         rows = pl.ds(pl.multiple_of(i * ROWS, ROWS), ROWS)
+        slot = (i % 2) * 4 + i // 2
         key_part = product(s1h, s1l, wh[0], wl[0], rows) + product(s2h, s2l, wh[1], wl[1], rows)
         key_part += product(s4h, s4l, nh[0], nl[0], rows) + product(s5h, s5l, nh[1], nl[1], rows)
         value_part = product(s3h, s3l, wh[2], wl[2], rows) + product(s6h, s6l, nh[2], nl[2], rows)
-        dkv[i, 0:ROWS, 0:HD] = key_part
-        dkv[i, 0:ROWS, HD:2 * HD] = value_part
+        dkv[slot, 0:ROWS, 0:HD] = key_part
+        dkv[slot, 0:ROWS, HD:2 * HD] = value_part
         return 0
 
-    lax.fori_loop(0, SLOTS, key_chunk, 0)
-    for s in range(SLOTS):
-        dkv[s, ROWS:ROWS + 8, :] = jnp.zeros((8, 2 * HD), f32)
-        lane = (s % 2) * ROWS
-        dkv[s, ROWS:ROWS + 8, 0:ROWS] = rate_rows[s // 2, :, lane:lane + ROWS] + d_totals
-    pair = send(dkv.at[pl.ds(4, 4)], xkv, peer("core", 1))
-
-    total = f_t[pl.ds(pl.multiple_of(x * x_rows, x_rows), x_rows), :]
-    for d in range(1, NX):
-        weight_copies[d - 1].wait_recv()
-        total = total + f_r1[d - 1]
-    for n in range(NZ):
-        f_s1[n, 0:GROUP, :] = total[GROUP * n:GROUP * (n + 1), :]
-        f_s1[n, GROUP:8, :] = jnp.zeros((8 - GROUP, 640), f32)
-    weight_copies = [send(f_s1.at[(z + d) % NZ], f_r2.at[d - 1], peer("z", d)) for d in range(1, NZ)]
-    row_back = return_rows(pair, dkv, xkv, okv, rkv)
-
+    with jax.named_scope("row_grads"):
+        lax.fori_loop(0, SLOTS, key_chunk, 0)
+        for s in range(SLOTS):
+            dkv[s, ROWS:ROWS + 8, :] = jnp.zeros((8, 2 * HD), f32)
+            lane = (s // 4) * ROWS
+            dkv[s, ROWS:ROWS + 8, 0:ROWS] = rate_rows[s % 4, :, lane:lane + ROWS] + d_totals
+        pair = send(dkv.at[pl.ds(4, 4)], xkv, peer("core", 1))
+
+    with jax.named_scope("x_sums"):
+        total = f_t[pl.ds(pl.multiple_of(x * x_rows, x_rows), x_rows), :]
+        for d in range(1, NX):
+            weight_copies[d - 1].wait_recv()
+            total = total + f_r1[d - 1]
+        for n in range(NZ):
+            f_s1[n, 0:GROUP, :] = total[GROUP * n:GROUP * (n + 1), :]
+            f_s1[n, GROUP:8, :] = jnp.zeros((8 - GROUP, 640), f32)
+        weight_copies = [send(f_s1.at[(z + d) % NZ], f_r2.at[d - 1], peer("z", d)) for d in range(1, NZ)]
+    with jax.named_scope("row_returns"):
+        row_back = return_rows(pair, dkv, xkv, okv, rkv)
+    with jax.named_scope("direct"):
+        direct_tiles = lanes_of(*direct, jnp.zeros((HALF, 64), f32))
+        for j in range(5):
+            for n in range(HALF // GROUP):
+                d_grp[n, 0:GROUP, 128 * j:128 * (j + 1)] = direct_tiles[j][GROUP * n:GROUP * (n + 1), :]
+
+    z_scope = jax.named_scope("z_sums")
+    z_scope.__enter__()
     total = f_s1[z]
     for d in range(1, NZ):
         weight_copies[d - 1].wait_recv()
@@ -513,34 +567,52 @@
 
         far_copies.append(copy)
 
-    def rows_out(out_ref, landing, lanes):
+    z_scope.__exit__(None, None, None)
+
+    def rows_out(which, landing, lanes):
         for h in range(HEADS):
             d = (h + NY - y) % NY
-            out_ref[:, HD * h:HD * (h + 1)] = landing[d, 0:ROWS, lanes:lanes + HD].astype(bf16)
-
-    for copy in query_back:
-        copy.wait_recv()
-    rows_out(qg_out, rq, 0)
-    for copy in row_back:
-        copy.wait_recv()
-    rows_out(kg_out, rkv, 0)
-    rows_out(vg_out, rkv, HD)
-    for h in range(HEADS):
-        rg_out[h] = rkv[(h + NY - y) % NY, ROWS:ROWS + 8, 0:ROWS]
-
+            rows_ref[which, :, HD * h:HD * (h + 1)] = landing[d, 0:ROWS, lanes:lanes + HD].astype(bf16)
+
+    with jax.named_scope("query_rows"):
+        for copy in query_back:
+            copy.wait_recv()
+        rows_out(0, rq, 0)
+    with jax.named_scope("key_rows"):
+        for copy in row_back:
+            copy.wait_recv()
+        rows_out(1, rkv, 0)
+        rows_out(2, rkv, HD)
+        for h in range(HEADS):
+            rg_out[h:h + 1, :] = rkv[(h + NY - y) % NY, ROWS:ROWS + 1, 0:ROWS]
+
+    with jax.named_scope("columns"):
+        for m in range(3):
+            @pl.when(near_index[m] != mine)
+            def _():
+                pltpu.make_async_remote_copy(
+                    src_ref=f_msg.at[m], dst_ref=fg_out.at[m], send_sem=far_sems.at[0, m],
+                    recv_sem=far_sems.at[1, m], device_id=(view, patch), device_id_type=MESH,
+                ).wait_recv()
+
+            @pl.when(far_owner[m] != mine)
+            def _():
+                far_copies[m].wait_send()
+        for copy in started:
+            copy.wait_send()
+
+
+def finish(rows, rate_rows, groups, query_out, key_out, value_out, rate_out, fast_out, sems):
+    copies = [
+        pltpu.make_async_copy(rows.at[n], out, sems.at[n]) for n, out in enumerate((query_out, key_out, value_out))
+    ]
+    for copy in copies:
+        copy.start()
+    rate_out[...] = rate_rows[...]
     for m in range(3):
-        @pl.when(near_index[m] != mine)
-        def _():
-            pltpu.make_async_remote_copy(
-                src_ref=f_msg.at[m], dst_ref=fg_out.at[m], send_sem=far_sems.at[0, m], recv_sem=far_sems.at[1, m],
-                device_id=(view, patch), device_id_type=MESH,
-            ).wait_recv()
-
-        @pl.when(far_owner[m] != mine)
-        def _():
-            far_copies[m].wait_send()
-    for copy in started:
-        copy.wait_send()
+        fast_out[GROUP * m:GROUP * (m + 1), :] = groups[m, 0:GROUP, 0:HD]
+    for copy in copies:
+        copy.wait()
 
 
 def scratch():
@@ -553,9 +625,9 @@
         pltpu.VMEM((3, 2, HALF, 1), f32),
         *[pltpu.VMEM((HEADS, ROWS + 8, 2 * HD), f32)] * 2,
         *[pltpu.VMEM((SLOTS, ROWS + 8, 2 * HD), f32)] * 2,
-        pltpu.VMEM((ALL_ROWS, 1), f32),
+        *[pltpu.VMEM((ALL_ROWS, 1), f32)] * 2,
         *[pltpu.VMEM((ALL_ROWS, HD), bf16)] * 4,
-        *[pltpu.VMEM((ALL_ROWS, HALF), f32)] * 3,
+        *[pltpu.VMEM((ALL_ROWS, HALF), f32)] * 7,
         *[pltpu.VMEM((ALL_ROWS, HALF), bf16)] * 12,
         pltpu.VMEM((3, HALF, HD), f32),
         pltpu.VMEM((ALL_ROWS // CHUNK, 8, CHUNK), f32),
@@ -593,25 +665,33 @@
 
 def on_device(queries, key_rows, value_rows, step_rates, fast_init, out_grad):
     vmem = pl.BlockSpec(memory_space=pltpu.VMEM)
-    rows = jax.ShapeDtypeStruct((ROWS, HEADS * HD), bf16)
-    query_grad, key_grad, value_grad, rate_tiles, groups = pl.pallas_call(
+    anywhere = pl.BlockSpec(memory_space=pl.ANY)
+    rates_shape = jax.ShapeDtypeStruct((HEADS, ROWS), f32)
+    results = pl.pallas_call(
         kernel,
         out_shape=(
-            rows, rows, rows,
-            jax.ShapeDtypeStruct((HEADS, 8, ROWS), f32),
+            jax.ShapeDtypeStruct((3, ROWS, HEADS * HD), bf16),
+            rates_shape,
             jax.ShapeDtypeStruct((3, 8, 256), f32),
         ),
-        in_specs=[vmem] * 5 + [pl.BlockSpec(memory_space=pl.ANY)],
-        out_specs=(vmem,) * 5,
+        in_specs=[vmem] * 5 + [anywhere],
+        out_specs=(vmem,) * 3,
         scratch_shapes=scratch(),
         compiler_params=pltpu.CompilerParams(
             collective_id=0, has_side_effects=True, vmem_limit_bytes=56 * 2**20
         ),
         name="layer_grad",
     )(queries, key_rows, value_rows, step_rates.T, out_grad, fast_init)
-    rate_grad = rate_tiles[:, 0, :].T
-    fast_grad = groups[:, :GROUP, :HD].reshape(3 * GROUP, HD).T
-    return query_grad, key_grad, value_grad, rate_grad, fast_grad
+    rows = jax.ShapeDtypeStruct((ROWS, HEADS * HD), bf16)
+    query_grad, key_grad, value_grad, rate_grad, fast_grad = pl.pallas_call(
+        finish,
+        out_shape=(rows, rows, rows, rates_shape, jax.ShapeDtypeStruct((3 * GROUP, HD), f32)),
+        in_specs=[vmem] * 3,
+        out_specs=(anywhere,) * 3 + (vmem,) * 2,
+        scratch_shapes=[pltpu.SemaphoreType.DMA((3,))],
+        name="outputs",
+    )(*results)
+    return query_grad, key_grad, value_grad, rate_grad.T, fast_grad.T
 
 
 def solution(mesh):

time: 117 us -> 108 us (0.923); the launches traced: 115 us -> 108 us
  local copies, waits for them, and re-layouts: 7.49 us -> 0 us
    unnamed x3 -> x0, local copies, waits for them, and re-layouts: 4.85 us -> none
    reshape x1 -> x0, local copies, waits for them, and re-layouts: 1.35 us -> none  [on_device(): fast_grad = groups[:, :GROUP, :HD].reshape(3 * GROUP, HD).T]
    slice x1 -> x0, local copies, waits for them, and re-layouts: 1.3 us -> none  [on_device(): rate_grad = rate_tiles[:, 0, :].T]
    pallas_call x1 -> x2, Pallas kernels: 107 us -> 107 us  [the longest x1 105 us: on_device(): pl.pallas_call(kernel, out_shape=(jax.ShapeDtypeStruct((3, ROWS, HEADS *...]
where the time goes in v2:
time: 108 us
  Pallas kernels  107 us (99%)
    pallas_call x1, Pallas kernels, on_device(): pl.pallas_call(kernel, out_shape=(jax.ShapeDtypeStruct((3, ROWS, HEADS *...  105 us
    pallas_call x1, Pallas kernels, on_device(): pl.pallas_call(finish, out_shape=(rows, rows, rows, rates_shape, jax.Shap...  2.51 us

profile of v2, /device:TPU:1, one launch (start us, length us, event | category | flops | bytes accessed | tf_op | source)
XLA Modules:
  0.0 107.9 jit_solution(1802692158848566794)
XLA Ops:
  0.6 104.8 %layer_grad.1 = (bf16[3,128,768]{2,1,0:T(8,128)(2,1)}, f32[4,128]{1,0:T(4,128)}, f32[3,8,256]{2,1,0:T(8,128)}) custom-call(bf16[128,768]{1,0:T(8,128)(2,1)} %q_ref.1, bf16[128,768]{1,0:T(8,128)(2,1)} %k_ref.1, bf16[128,768]{1,0:T(8,128)(2,1)} %v_ref.1, f32[4,128]{1,0:T(4,128)} %bitcast.3, bf16[128,768]{1,0:T(8,128)(2,1)} %g_ref.1, f32[192,4608]{1,0:T(8,128)} %w_hbm.1), custom_call_target="tpu_custom_call" | custom-call | tf_op jit(solution)/shard_map/layer_grad/pallas_call | solution.py:670
  105.4 2.5 %outputs.1 = (bf16[128,768]{1,0:T(8,128)(2,1)}, bf16[128,768]{1,0:T(8,128)(2,1)}, bf16[128,768]{1,0:T(8,128)(2,1)}, f32[4,128]{1,0:T(4,128)}, f32[18,192]{1,0:T(8,128)}) custom-call(bf16[3,128,768]{2,1,0:T(8,128)(2,1)} %get-tuple-element.13.rows, f32[4,128]{1,0:T(4,128)} %get-tuple-element.14.rate_rows, f32[3,8,256]{2,1,0:T(8,128)} %get-tuple-element.15.groups), custom_call_target="tpu_custom_call" | custom-call | tf_op jit(solution)/shard_map/outputs/pallas_call | solution.py:686

commit v3 on v2

v3 whole, which is shorter than its diff:
```python
import itertools
import math

import jax
import jax.numpy as jnp
from jax import lax
from jax.experimental import pallas as pl
from jax.experimental.pallas import tpu as pltpu
from jax.sharding import PartitionSpec as P

MESH = pl.DeviceIdType.MESH
f32, bf16 = jnp.float32, jnp.bfloat16

step_size = 0.2
epsilon = 1e-06

NX, NY, NZ = 4, 4, 8
HEADS, HD, FF = 4, 192, 384
HALF = FF // 2
ROWS = 128
SLOTS = 8
ALL_ROWS = SLOTS * ROWS
CHUNK = 256
TOTAL_ROWS = ROWS * NX * NY * NZ * 2
COEFFICIENT = step_size * math.sqrt(TOTAL_ROWS)
N_SEMS = 240
GROUP = 6


def device(x, y, z, core):
    return ((x // 2) * 2 + core, (y * 2 + x % 2) * 8 + z)


BLOCKS = 2
UNITS = HALF // BLOCKS
PAD = 128
ROW_TILES = UNITS // 8
PIECE = UNITS // NX

PARTS = (("x", (0, 1, 2)), ("z", (3, 4)))


def part_sizes(part):
    axis, lane_tiles = part
    first, second = (NX, NZ) if axis == "x" else (NZ, NX)
    shard = ROW_TILES * len(lane_tiles) // first
    window = -(-shard // second)
    if (shard - window) // (second - 1) >= window and shard > second:
        window += 1
    return first, second, shard, window


def nt(a, b):
    return lax.dot_general(a, b, (((1,), (1,)), ((), ())), preferred_element_type=f32)


def nn(a, b):
    return lax.dot_general(a, b, (((1,), (0,)), ((), ())), preferred_element_type=f32)


def tn(a, b):
    return lax.dot_general(a, b, (((0,), (0,)), ((), ())), preferred_element_type=f32)


def split(value):
    high = value.astype(bf16)
    return high, (value - high.astype(f32)).astype(bf16)


def kernel(
    q_hbm, k_hbm, v_hbm, r_ref, g_hbm, w_hbm,
    rows_ref, rg_out, fg_out,
    q_ref, k_ref, v_ref, g_ref,
    w_load, w_own, wh_ab, wl_ab, nh_ab, nl_ab, wh_c, wl_c, nh_c, nl_c, moved, gm, norms,
    kv_send, qg_send, kv, qg, rates, inv_rates, kb, vb, qb, gb,
    gate_s, up_s, pull_s, m1, m2, m3, m4,
    s_ab_h, s_ab_l, e_ab_h, e_ab_l, s_c_h, s_c_l, e_c_h, e_c_l,
    acc_ab, acc_c, rate_rows, dq, xq, oq, rq, dkv, xkv, okv, rkv,
    p0_t, p0_r1, p0_s1, p0_r2, p0_s2, p0_a1, p0_f1, p0_g,
    p1_t, p1_r1, p1_s1, p1_r2, p1_s2, p1_a1, p1_f1, p1_g,
    f_t, f_r1, f_s1, f_r2, d_grp, f_msg,
    send_sems, recv_sems, far_sems, load_sems,
):
    view, patch = lax.axis_index("view"), lax.axis_index("patch")
    x, core = (view // 2) * 2 + (patch // 8) % 2, view % 2
    y, z = patch // 16, patch % 8
    mine = view * 64 + patch
    half_block = 2 * y + core

    def peer(axis, offset):
        if axis == "x":
            return device((x + offset) % NX, y, z, core)
        if axis == "y":
            return device(x, (y + offset) % NY, z, core)
        if axis == "z":
            return device(x, y, (z + offset) % NZ, core)
        return device(x, y, z, 1 - core)

    place = {"x": x, "z": z}

    far_group = [32 * (8 * m + half_block) + 8 * x + z for m in range(3)]
    far_owner = [group // 3 for group in far_group]
    near_source = []
    for t in range(3):
        group = 3 * mine + t
        block, rest = group // 32, group % 32
        near_source.append((rest // 8, (block % 8) // 2, rest % 8, block % 2))
    near_index = []
    for sx, sy, sz, sc in near_source:
        sv, sp = device(sx, sy, sz, sc)
        near_index.append(sv * 64 + sp)

    barrier = pltpu.get_barrier_semaphore()
    peers = [("x", d) for d in range(1, NX)] + [("z", d) for d in range(1, NZ)]
    peers += [("y", d) for d in range(1, NY)] + [("core", 1)]
    for axis, offset in peers:
        pl.semaphore_signal(barrier, inc=1, device_id=peer(axis, offset), device_id_type=MESH)
    for t in range(3):
        @pl.when(near_index[t] != mine)
        def _():
            pl.semaphore_signal(barrier, inc=1, device_id=device(*near_source[t]), device_id_type=MESH)

    ids = itertools.count()
    started = []

    def send(src, dst, target):
        which = next(ids)
        copy = pltpu.make_async_remote_copy(
            src_ref=src, dst_ref=dst, send_sem=send_sems.at[which], recv_sem=recv_sems.at[which],
            device_id=target, device_id_type=MESH,
        )
        copy.start()
        started.append(copy)
        return copy

    row_loads = []
    for n, (src, dst) in enumerate(((k_hbm, k_ref), (v_hbm, v_ref), (q_hbm, q_ref), (g_hbm, g_ref))):
        load = pltpu.make_async_copy(src, dst, load_sems.at[3 + n])
        load.start()
        row_loads.append(load)
    loads = []
    for m in range(3):
        first = pl.multiple_of(m * HEADS * FF + y * FF, 128)
        load = pltpu.make_async_copy(w_hbm.at[:, pl.ds(first, FF)], w_load.at[m], load_sems.at[m])
        load.start()
        loads.append(load)

    def pack(buffer, left, right):
        for h in range(HEADS):
            cols = slice(HD * h, HD * (h + 1))
            buffer[h, 0:ROWS, 0:HD] = left[:, cols].astype(f32)
            buffer[h, 0:ROWS, HD:2 * HD] = right[:, cols].astype(f32)

    row_loads[0].wait()
    row_loads[1].wait()
    pack(kv_send, k_ref, v_ref)
    for h in range(HEADS):
        kv_send[h, ROWS:ROWS + 8, :] = jnp.zeros((8, 2 * HD), f32)
        kv_send[h, ROWS:ROWS + 8, 0:ROWS] = jnp.broadcast_to(r_ref[h:h + 1, :], (8, ROWS))

    far_count = sum((owner != mine).astype(jnp.int32) for owner in far_owner)
    pl.semaphore_wait(barrier, len(peers) + far_count)

    def scatter_heads(buffer, landing):
        out = {}
        for d in (1, 3, 2):
            out[d] = send(buffer.at[(y + d) % NY], landing.at[d], peer("y", d))
        out["own"] = send(buffer.at[y], landing.at[4], peer("core", 1))
        return out

    kv_copies = scatter_heads(kv_send, kv)
    row_loads[2].wait()
    row_loads[3].wait()
    pack(qg_send, q_ref, g_ref)

    def store_weights(ab_h, ab_l, c_h, c_l, b, m, value):
        if m < 2:
            rows = (b, slice(PAD * m, PAD * m + UNITS))
            ab_h[rows], ab_l[rows] = split(value)
        else:
            rows = (b, slice(0, UNITS))
            c_h[rows], c_l[rows] = split(value)

    for b in range(BLOCKS):
        none = jnp.zeros((PAD - UNITS, HD), bf16)
        for ref in (wh_ab, wl_ab, nh_ab, nl_ab):
            ref[b, UNITS:PAD] = none
            ref[b, PAD + UNITS:2 * PAD] = none
        for ref in (wh_c, wl_c, nh_c, nl_c):
            ref[b, UNITS:PAD] = none
    for m in range(3):
        loads[m].wait()
        both = w_load[m]
        own = jnp.where(core == 0, both[:, 0:HALF], both[:, HALF:FF]).T
        for b in range(BLOCKS):
            pieces = [own[2 * PIECE * n + PIECE * b:2 * PIECE * n + PIECE * (b + 1), :] for n in range(NX)]
            block = jnp.concatenate(pieces, axis=0)
            w_own[b, m] = block
            norms[b, m, 0] = jnp.sqrt(jnp.sum(block * block, axis=1, keepdims=True) + epsilon)
            store_weights(wh_ab, wl_ab, wh_c, wl_c, b, m, block)

    def row_block(s):
        first = (s % 4) * CHUNK + (s // 4) * ROWS
        return slice(first, first + ROWS)

    def unpack_kv(s):
        kb[row_block(s), :] = kv[s, 0:ROWS, 0:HD].astype(bf16)
        vb[row_block(s), :] = kv[s, 0:ROWS, HD:2 * HD].astype(bf16)
        column = kv[s, ROWS:ROWS + 8, 0:ROWS].T[:, 0:1]
        rates[row_block(s), :] = column
        inv_rates[row_block(s), :] = 1.0 / column

    def unpack_qg(s):
        qb[row_block(s), :] = qg[s, 0:ROWS, 0:HD].astype(bf16)
        gb[row_block(s), :] = qg[s, 0:ROWS, HD:2 * HD].astype(bf16)

    def silu_parts(gate):
        sig = 1.0 / (1.0 + jnp.exp(-gate))
        act = gate * sig
        slope = sig + act * (1.0 - sig)
        return sig, act, slope

    def clear(b):
        acc_ab[b] = jnp.zeros((2 * PAD, HD), f32)
        acc_c[b] = jnp.zeros((PAD, HD), f32)

    for b in range(BLOCKS):
        clear(b)

    GATE, UP = slice(0, PAD), slice(PAD, 2 * PAD)

    def add_terms(b, rows, gate_term, up_term, pull_term, left, right):
        s_ab_h[b, rows, GATE], s_ab_l[b, rows, GATE] = split(gate_term)
        s_ab_h[b, rows, UP], s_ab_l[b, rows, UP] = split(up_term)
        s_c_h[b, rows, :], s_c_l[b, rows, :] = split(pull_term)
        acc_ab[b] += tn(s_ab_h[b, rows, :], left) + tn(s_ab_l[b, rows, :], left)
        acc_c[b] += tn(s_c_h[b, rows, :], right) + tn(s_c_l[b, rows, :], right)

    def update_chunk(b, i):
        rows = slice(i * CHUNK, (i + 1) * CHUNK)
        keys, values, eta = kb[rows, :], vb[rows, :], rates[rows, :]
        both = nt(keys, wh_ab[b]) + nt(keys, wl_ab[b])
        gate, up = both[:, GATE], both[:, UP]
        pulled = nt(values, wh_c[b]) + nt(values, wl_c[b])
        gate_s[b, rows, :], up_s[b, rows, :], pull_s[b, rows, :] = gate, up, pulled
        _, act, slope = silu_parts(gate)
        scaled = -eta * pulled
        add_terms(b, rows, scaled * up * slope, scaled * act, -eta * act * up, keys, values)

    def take_pair(d):
        unpack_kv(d)
        unpack_kv(4 + d)

    def pass_on(copies, landing, d):
        copies[d].wait_recv()
        return send(landing.at[d], landing.at[4 + d], peer("core", 1))

    with jax.named_scope("keys_own"):
        kv[0] = kv_send[y]
        kv_copies["own"].wait_recv()
        take_pair(0)
        for b in range(BLOCKS):
            update_chunk(b, 0)
    passed = {}
    with jax.named_scope("keys_first"):
        passed[1] = pass_on(kv_copies, kv, 1)
        passed[3] = pass_on(kv_copies, kv, 3)
        passed[1].wait_recv()
        take_pair(1)
        for b in range(BLOCKS):
            update_chunk(b, 1)
    with jax.named_scope("keys_second"):
        passed[2] = pass_on(kv_copies, kv, 2)
        qg_copies = scatter_heads(qg_send, qg)
        passed[3].wait_recv()
        take_pair(3)
        for b in range(BLOCKS):
            update_chunk(b, 3)
    with jax.named_scope("keys_third"):
        passed[2].wait_recv()
        take_pair(2)

    rate_sum = sum(kv[s, ROWS:ROWS + 8, 0:ROWS] for s in range(SLOTS))
    total_part = jnp.sum(rate_sum[0:1, :], axis=1, keepdims=True)

    parts = (
        (p0_t, p0_r1, p0_s1, p0_r2, p0_s2, p0_a1, p0_f1, p0_g),
        (p1_t, p1_r1, p1_s1, p1_r2, p1_s2, p1_a1, p1_f1, p1_g),
    )

    def lanes_of(first, second, third, tail):
        return (
            first[:, 0:128],
            second[:, 0:128],
            jnp.concatenate([first[:, 128:192], second[:, 128:192]], axis=1),
            third[:, 0:128],
            jnp.concatenate([third[:, 128:192], tail], axis=1),
        )

    def sums_of(b, tail):
        return lanes_of(
            acc_ab[b, 0:UNITS, :], acc_ab[b, PAD:PAD + UNITS, :], acc_c[b, 0:UNITS, :], tail
        )

    def start_stage(r, p, source):
        axis, lane_tiles = PARTS[p]
        first, second, shard, window = part_sizes(PARTS[p])
        t = parts[p][0]
        for jj, j in enumerate(lane_tiles):
            t[r, jj * ROW_TILES:(jj + 1) * ROW_TILES] = source[j].reshape(ROW_TILES, 8, 128)
        copies = []
        for d in range(1, first):
            there = (place[axis] + d) % first
            copies.append(send(t.at[r, pl.ds(there * shard, shard)], parts[p][1].at[r, d - 1], peer(axis, d)))
        return copies

    def start_of(p, k):
        _, second, shard, window = part_sizes(PARTS[p])
        return ((shard - window) * k) // (second - 1)

    def second_stage(r, p, copies):
        axis = PARTS[p][0]
        other = "z" if axis == "x" else "x"
        first, second, shard, window = part_sizes(PARTS[p])
        t, r1, s1, r2 = parts[p][:4]
        total = t[r, pl.ds(place[axis] * shard, shard)]
        for d in range(1, first):
            copies[d - 1].wait_recv()
            total = total + r1[r, d - 1]
        s1[r] = total
        out = []
        for d in range(1, second):
            there = (place[other] + d) % second
            out.append(send(s1.at[r, pl.ds(start_of(p, there), window)], r2.at[r, d - 1], peer(other, d)))
        return out

    def third_stage(r, p, copies):
        other = "z" if PARTS[p][0] == "x" else "x"
        _, second, shard, window = part_sizes(PARTS[p])
        _, _, s1, r2, s2, a1, f1, _ = parts[p]
        total = s1[r, pl.ds(start_of(p, place[other]), window)]
        for d in range(1, second):
            copies[d - 1].wait_recv()
            total = total + r2[r, d - 1]
        s2[r] = total
        return [send(s2.at[r], a1.at[r, d - 1], peer(other, d)) for d in range(1, second)]

    def fourth_stage(r, p, copies):
        axis = PARTS[p][0]
        other = "z" if axis == "x" else "x"
        first, second, shard, window = part_sizes(PARTS[p])
        _, _, _, _, s2, a1, f1, g = parts[p]
        f1[r, pl.ds(start_of(p, place[other]), window)] = s2[r]
        for d in range(1, second):
            copies[d - 1].wait_recv()
            there = (place[other] + second - d) % second
            f1[r, pl.ds(start_of(p, there), window)] = a1[r, d - 1]
        here = pl.ds(place[axis] * shard, shard)
        out = [send(f1.at[r], g.at[r, here], peer(axis, d)) for d in range(1, first)]
        g[r, here] = f1[r]
        return out

    class Sum:
        def __init__(self, r, b):
            self.r = 2 * r + b
            self.b = b

        def start(self, tail):
            source = sums_of(self.b, tail)
            self.copies = [start_stage(self.r, p, source) for p in (1, 0)][::-1]

        def step(self, stage):
            self.copies = [stage(self.r, p, self.copies[p]) for p in range(2)]

        def result(self):
            for group in self.copies:
                for copy in group:
                    copy.wait_recv()
            tiles = {}
            for p in range(2):
                for jj, j in enumerate(PARTS[p][1]):
                    tiles[j] = parts[p][7][self.r, jj * ROW_TILES:(jj + 1) * ROW_TILES].reshape(UNITS, 128)
            gate = jnp.concatenate([tiles[0], tiles[2][:, 0:64]], axis=1)
            up = jnp.concatenate([tiles[1], tiles[2][:, 64:128]], axis=1)
            down = jnp.concatenate([tiles[3], tiles[4][:, 0:64]], axis=1)
            return (gate, up, down), tiles[4][0:1, 64:65]

    def prepare_chunk(i, _):
        rows = pl.ds(pl.multiple_of(i * CHUNK, CHUNK), CHUNK)
        eta = rates[rows, :]
        for b in range(BLOCKS):
            gate, up, pulled = gate_s[b, rows, :], up_s[b, rows, :], pull_s[b, rows, :]
            sig, act, slope = silu_parts(gate)
            curve = sig * (1.0 - sig) * (2.0 + gate * (1.0 - 2.0 * sig))
            scaled = eta * pulled
            by_slope, by_act = eta * (up * slope), eta * act
            m1[b, rows, :], m2[b, rows, :] = scaled * up * curve, scaled * slope
            m3[b, rows, :], m4[b, rows, :] = by_slope, by_act
            e_ab_h[b, rows, GATE], e_ab_l[b, rows, GATE] = split(by_slope * pulled)
            e_ab_h[b, rows, UP], e_ab_l[b, rows, UP] = split(by_act * pulled)
            e_c_h[b, rows, :], e_c_l[b, rows, :] = split(by_act * up)
        return 0

    query_passed = {}

    def prepare():
        lax.fori_loop(0, ALL_ROWS // CHUNK, prepare_chunk, 0)

    def pass_queries():
        qg[0] = qg_send[y]
        for d in (1, 3, 2):
            query_passed[d] = pass_on(qg_copies, qg, d)

    def take_queries():
        qg_copies["own"].wait_recv()
        for d in (1, 3, 2):
            query_passed[d].wait_recv()
        for s in range(SLOTS):
            unpack_qg(s)

    tail = jnp.broadcast_to(total_part, (UNITS, 64))
    sums = [Sum(0, b) for b in range(BLOCKS)]
    for b in range(BLOCKS):
        with jax.named_scope("keys_last"):
            update_chunk(b, 2)
            sums[b].start(tail)
    prepare()
    for stage, work in ((second_stage, pass_queries), (third_stage, take_queries), (fourth_stage, None)):
        for b in range(BLOCKS):
            sums[b].step(stage)
        if work is not None:
            work()

    def new_weights(b):
        terms, total = sums[b].result()
        scale = COEFFICIENT / total
        for m in range(3):
            change = terms[m] * scale
            shifted = w_own[b, m] - change
            inverse = lax.rsqrt(jnp.sum(shifted * shifted, axis=1, keepdims=True) + epsilon)
            gm[b, m], moved[b, m], norms[b, m, 1] = change, shifted, inverse
            store_weights(nh_ab, nl_ab, nh_c, nl_c, b, m, shifted * (norms[b, m, 0] * inverse))
        clear(b)
        return total, scale

    def apply_block(b):
        def apply_chunk(i, _):
            rows = pl.ds(pl.multiple_of(i * CHUNK, CHUNK), CHUNK)
            queries, grads = qb[rows, :], gb[rows, :]
            both = nt(queries, nh_ab[b]) + nt(queries, nl_ab[b])
            gate, up = both[:, GATE], both[:, UP]
            pulled = nt(grads, nh_c[b]) + nt(grads, nl_c[b])
            _, act, slope = silu_parts(gate)
            add_terms(b, rows, pulled * up * slope, pulled * act, act * up, queries, grads)
            return 0

        lax.fori_loop(0, ALL_ROWS // CHUNK, apply_chunk, 0)

    new_sums = [Sum(1, b) for b in range(BLOCKS)]
    for b in range(BLOCKS):
        with jax.named_scope("apply"):
            totals, scale = new_weights(b)
            apply_block(b)
            new_sums[b].start(jnp.zeros((UNITS, 64), f32))

    def product(ah, al, bh, bl, rows):
        high = ah[rows, :]
        return nn(high, bh) + nn(high, bl) + nn(al[rows, :], bh)

    def query_grads(b):
        def query_chunk(i, _):
            rows = pl.ds(pl.multiple_of(i * ROWS, ROWS), ROWS)
            slot = (i % 2) * 4 + i // 2
            part = product(s_ab_h.at[b], s_ab_l.at[b], nh_ab[b], nl_ab[b], rows)
            dq[slot] = part if b == 0 else dq[slot] + part
            return 0

        lax.fori_loop(0, SLOTS, query_chunk, 0)

    def return_rows(pair, partial, arrived, sums, landing):
        pair.wait_recv()
        out = []
        for d in (1, 3, 2, 0):
            if d == 0:
                landing[0] = partial[0] + arrived[0]
            else:
                sums[d] = partial[d] + arrived[d]
                out.append(send(sums.at[d], landing.at[d], peer("y", NY - d)))
        return out

    for b in range(BLOCKS):
        with jax.named_scope("query_grads"):
            query_grads(b)
        new_sums[b].step(second_stage)
    query_pair = send(dq.at[pl.ds(4, 4)], xq, peer("core", 1))
    new_sums[0].step(third_stage)
    query_back = return_rows(query_pair, dq, xq, oq, rq)
    new_sums[1].step(third_stage)
    for b in range(BLOCKS):
        new_sums[b].step(fourth_stage)

    direct = {}

    def pull_weights(b):
        d_new, _ = new_sums[b].result()
        head_part = jnp.zeros((1, 1), f32)
        for m in range(3):
            init_norm, inverse = norms[b, m, 0], norms[b, m, 1]
            shifted = moved[b, m]
            dots = jnp.sum(d_new[m] * shifted, axis=1, keepdims=True)
            d_moved = d_new[m] * (init_norm * inverse) - shifted * (dots * init_norm * inverse * inverse * inverse)
            direct[b, m] = d_moved + w_own[b, m] * (dots * inverse / init_norm)
            by_row = jnp.sum(d_moved * gm[b, m], axis=1, keepdims=True)
            head_part = head_part - jnp.sum(by_row, axis=0, keepdims=True)
            store_weights(nh_ab, nl_ab, nh_c, nl_c, b, m, d_moved * scale)
        clear(b)
        return -head_part / totals

    def pull_block(b):
        def pull_chunk(i, _):
            rows = pl.ds(pl.multiple_of(i * CHUNK, CHUNK), CHUNK)
            keys, values = kb[rows, :], vb[rows, :]
            both = nt(keys, nh_ab[b]) + nt(keys, nl_ab[b])
            one, two = both[:, GATE], both[:, UP]
            three = nt(values, nh_c[b]) + nt(values, nl_c[b])
            by_slope, by_act, by_two = m3[b, rows, :], m4[b, rows, :], m2[b, rows, :]
            c_gate = one * m1[b, rows, :] + two * by_two + three * by_slope
            c_up = one * by_two + three * by_act
            c_pull = one * by_slope + two * by_act
            add_terms(b, rows, c_gate, c_up, c_pull, keys, values)
            by_rate = c_pull * pull_s[b, rows, :] + three * (by_act * up_s[b, rows, :])
            by_rate_h, by_rate_l = split(by_rate * inv_rates[rows, :])
            ones = jnp.ones((8, PAD), bf16)
            part = nt(ones, by_rate_h) + nt(ones, by_rate_l)
            rate_rows[i] = part if b == 0 else rate_rows[i] + part
            return 0

        lax.fori_loop(0, ALL_ROWS // CHUNK, pull_chunk, 0)

    weight_copies = []
    d_totals = jnp.zeros((1, 1), f32)
    for b in range(BLOCKS):
        with jax.named_scope("pull"):
            d_totals = d_totals + pull_weights(b)
            pull_block(b)
            tiles = sums_of(b, jnp.zeros((UNITS, 64), f32))
            for j in range(5):
                f_t[b, :, 128 * j:128 * (j + 1)] = tiles[j]
            for d in range(1, NX):
                first = pl.multiple_of(((x + d) % NX) * PIECE, PIECE)
                weight_copies.append(send(f_t.at[b, pl.ds(first, PIECE)], f_r1.at[b, d - 1], peer("x", d)))

    def key_chunk(i, _):
        rows = pl.ds(pl.multiple_of(i * ROWS, ROWS), ROWS)
        slot = (i % 2) * 4 + i // 2
        key_part, value_part = 0.0, 0.0
        for b in range(BLOCKS):
            key_part += product(s_ab_h.at[b], s_ab_l.at[b], wh_ab[b], wl_ab[b], rows)
            key_part += product(e_ab_h.at[b], e_ab_l.at[b], nh_ab[b], nl_ab[b], rows)
            value_part += product(s_c_h.at[b], s_c_l.at[b], wh_c[b], wl_c[b], rows)
            value_part += product(e_c_h.at[b], e_c_l.at[b], nh_c[b], nl_c[b], rows)
        dkv[slot, 0:ROWS, 0:HD] = key_part
        dkv[slot, 0:ROWS, HD:2 * HD] = value_part
        return 0

    with jax.named_scope("row_grads"):
        lax.fori_loop(0, SLOTS, key_chunk, 0)
        for s in range(SLOTS):
            dkv[s, ROWS:ROWS + 8, :] = jnp.zeros((8, 2 * HD), f32)
            lane = (s // 4) * ROWS
            dkv[s, ROWS:ROWS + 8, 0:ROWS] = rate_rows[s % 4, :, lane:lane + ROWS] + d_totals
        pair = send(dkv.at[pl.ds(4, 4)], xkv, peer("core", 1))

    with jax.named_scope("x_sums"):
        for b in range(BLOCKS):
            total = f_t[b, pl.ds(pl.multiple_of(x * PIECE, PIECE), PIECE), :]
            for d in range(1, NX):
                weight_copies[(NX - 1) * b + d - 1].wait_recv()
                total = total + f_r1[b, d - 1]
            for n in range(4):
                f_s1[4 * b + n, 0:GROUP, :] = total[GROUP * n:GROUP * (n + 1), :]
                f_s1[4 * b + n, GROUP:8, :] = jnp.zeros((8 - GROUP, 640), f32)
        weight_copies = [send(f_s1.at[(z + d) % NZ], f_r2.at[d - 1], peer("z", d)) for d in range(1, NZ)]
    with jax.named_scope("row_returns"):
        row_back = return_rows(pair, dkv, xkv, okv, rkv)
    with jax.named_scope("direct"):
        for b in range(BLOCKS):
            tiles = lanes_of(direct[b, 0], direct[b, 1], direct[b, 2], jnp.zeros((UNITS, 64), f32))
            for j in range(5):
                for n in range(16):
                    group = 8 * (n // 4) + 4 * b + n % 4
                    d_grp[group, 0:GROUP, 128 * j:128 * (j + 1)] = tiles[j][GROUP * n:GROUP * (n + 1), :]

    z_scope = jax.named_scope("z_sums")
    z_scope.__enter__()
    total = f_s1[z]
    for d in range(1, NZ):
        weight_copies[d - 1].wait_recv()
        total = total + f_r2[d - 1]
    total = (total + d_grp[8 * x + z]) * (1.0 / math.sqrt(TOTAL_ROWS))
    for m, (low, high) in enumerate(((0, 256), (128, 320), (384, 512))):
        f_msg[m, :, 0:128] = total[:, low:low + 128]
        f_msg[m, :, 128:HD] = total[:, high:high + 64]
    far_copies = []
    for m in range(3):
        slot = far_group[m] % 3
        owner = far_owner[m]
        copy = pltpu.make_async_remote_copy(
            src_ref=f_msg.at[m], dst_ref=fg_out.at[slot], send_sem=far_sems.at[0, m], recv_sem=far_sems.at[1, slot],
            device_id=(owner // 64, owner % 64), device_id_type=MESH,
        )

        @pl.when(owner != mine)
        def _():
            copy.start()

        @pl.when(owner == mine)
        def _():
            fg_out[slot] = f_msg[m]

        far_copies.append(copy)

    z_scope.__exit__(None, None, None)

    def rows_out(which, landing, lanes):
        for h in range(HEADS):
            d = (h + NY - y) % NY
            rows_ref[which, :, HD * h:HD * (h + 1)] = landing[d, 0:ROWS, lanes:lanes + HD].astype(bf16)

    with jax.named_scope("query_rows"):
        for copy in query_back:
            copy.wait_recv()
        rows_out(0, rq, 0)
    with jax.named_scope("key_rows"):
        for copy in row_back:
            copy.wait_recv()
        rows_out(1, rkv, 0)
        rows_out(2, rkv, HD)
        for h in range(HEADS):
            rg_out[h:h + 1, :] = rkv[(h + NY - y) % NY, ROWS:ROWS + 1, 0:ROWS]

    with jax.named_scope("columns"):
        for m in range(3):
            @pl.when(near_index[m] != mine)
            def _():
                pltpu.make_async_remote_copy(
                    src_ref=f_msg.at[m], dst_ref=fg_out.at[m], send_sem=far_sems.at[0, m],
                    recv_sem=far_sems.at[1, m], device_id=(view, patch), device_id_type=MESH,
                ).wait_recv()

            @pl.when(far_owner[m] != mine)
            def _():
                far_copies[m].wait_send()
        for copy in started:
            copy.wait_send()


def finish(rows, rate_rows, groups, query_out, key_out, value_out, rate_out, fast_out, sems):
    copies = [
        pltpu.make_async_copy(rows.at[n], out, sems.at[n]) for n, out in enumerate((query_out, key_out, value_out))
    ]
    for copy in copies:
        copy.start()
    rate_out[...] = rate_rows[...]
    for m in range(3):
        fast_out[GROUP * m:GROUP * (m + 1), :] = groups[m, 0:GROUP, 0:HD]
    for copy in copies:
        copy.wait()


def scratch():
    tile = (8, 128)
    halves = (BLOCKS, ALL_ROWS)
    shapes = [
        *[pltpu.VMEM((ROWS, HEADS * HD), bf16)] * 4,
        pltpu.VMEM((3, HD, FF), f32),
        pltpu.VMEM((BLOCKS, 3, UNITS, HD), f32),
        *[pltpu.VMEM((BLOCKS, 2 * PAD, HD), bf16)] * 4,
        *[pltpu.VMEM((BLOCKS, PAD, HD), bf16)] * 4,
        *[pltpu.VMEM((BLOCKS, 3, UNITS, HD), f32)] * 2,
        pltpu.VMEM((BLOCKS, 3, 2, UNITS, 1), f32),
        *[pltpu.VMEM((HEADS, ROWS + 8, 2 * HD), f32)] * 2,
        *[pltpu.VMEM((SLOTS, ROWS + 8, 2 * HD), f32)] * 2,
        *[pltpu.VMEM((ALL_ROWS, 1), f32)] * 2,
        *[pltpu.VMEM((ALL_ROWS, HD), bf16)] * 4,
        *[pltpu.VMEM(halves + (PAD,), f32)] * 7,
        *[pltpu.VMEM(halves + (2 * PAD,), bf16)] * 4,
        *[pltpu.VMEM(halves + (PAD,), bf16)] * 4,
        pltpu.VMEM((BLOCKS, 2 * PAD, HD), f32),
        pltpu.VMEM((BLOCKS, PAD, HD), f32),
        pltpu.VMEM((ALL_ROWS // CHUNK, 8, CHUNK), f32),
        pltpu.VMEM((SLOTS, ROWS, HD), f32),
        *[pltpu.VMEM((4, ROWS, HD), f32)] * 3,
        pltpu.VMEM((SLOTS, ROWS + 8, 2 * HD), f32),
        *[pltpu.VMEM((4, ROWS + 8, 2 * HD), f32)] * 3,
    ]
    rounds = 2 * BLOCKS
    for part in PARTS:
        first, second, shard, window = part_sizes(part)
        shapes += [
            pltpu.VMEM((rounds, first * shard) + tile, f32),
            pltpu.VMEM((rounds, first - 1, shard) + tile, f32),
            pltpu.VMEM((rounds, shard) + tile, f32),
            pltpu.VMEM((rounds, second - 1, window) + tile, f32),
            pltpu.VMEM((rounds, window) + tile, f32),
            pltpu.VMEM((rounds, second - 1, window) + tile, f32),
            pltpu.VMEM((rounds, shard) + tile, f32),
            pltpu.VMEM((rounds, first * shard) + tile, f32),
        ]
    shapes += [
        pltpu.VMEM((BLOCKS, UNITS, 640), f32),
        pltpu.VMEM((BLOCKS, NX - 1, PIECE, 640), f32),
        pltpu.VMEM((NZ, 8, 640), f32),
        pltpu.VMEM((NZ - 1, 8, 640), f32),
        pltpu.VMEM((HALF // GROUP, 8, 640), f32),
        pltpu.VMEM((3, 8, 256), f32),
        pltpu.SemaphoreType.DMA((N_SEMS,)),
        pltpu.SemaphoreType.DMA((N_SEMS,)),
        pltpu.SemaphoreType.DMA((2, 3)),
        pltpu.SemaphoreType.DMA((7,)),
    ]
    return shapes


def on_device(queries, key_rows, value_rows, step_rates, fast_init, out_grad):
    vmem = pl.BlockSpec(memory_space=pltpu.VMEM)
    anywhere = pl.BlockSpec(memory_space=pl.ANY)
    rates_shape = jax.ShapeDtypeStruct((HEADS, ROWS), f32)
    results = pl.pallas_call(
        kernel,
        out_shape=(
            jax.ShapeDtypeStruct((3, ROWS, HEADS * HD), bf16),
            rates_shape,
            jax.ShapeDtypeStruct((3, 8, 256), f32),
        ),
        in_specs=[anywhere] * 3 + [vmem] + [anywhere] * 2,
        out_specs=(vmem,) * 3,
        scratch_shapes=scratch(),
        compiler_params=pltpu.CompilerParams(
            collective_id=0, has_side_effects=True, vmem_limit_bytes=56 * 2**20
        ),
        name="layer_grad",
    )(queries, key_rows, value_rows, step_rates.T, out_grad, fast_init)
    rows = jax.ShapeDtypeStruct((ROWS, HEADS * HD), bf16)
    query_grad, key_grad, value_grad, rate_grad, fast_grad = pl.pallas_call(
        finish,
        out_shape=(rows, rows, rows, rates_shape, jax.ShapeDtypeStruct((3 * GROUP, HD), f32)),
        in_specs=[vmem] * 3,
        out_specs=(anywhere,) * 3 + (vmem,) * 2,
        scratch_shapes=[pltpu.SemaphoreType.DMA((3,))],
        name="outputs",
    )(*results)
    return query_grad, key_grad, value_grad, rate_grad.T, fast_grad.T


def solution(mesh):
    both = ("view", "patch")
    return jax.shard_map(
        on_device,
        mesh=mesh,
        in_specs=(P(both, None), P(both, None), P(both, None), P(both, None), P(), P(both, None)),
        out_specs=(P(both, None), P(both, None), P(both, None), P(both, None), P(None, both)),
        check_vma=False,
    )
```

time: 108 us -> 107 us (level)
    pallas_call x1, Pallas kernels: 105 us -> 103 us  [on_device(): pl.pallas_call(kernel, out_shape=(jax.ShapeDtypeStruct((3, ROWS, HEADS *...]
where the time goes in v3:
time: 107 us
  Pallas kernels  106 us (99%)
    pallas_call x1, Pallas kernels, on_device(): pl.pallas_call(kernel, out_shape=(jax.ShapeDtypeStruct((3, ROWS, HEADS *...  103 us
    pallas_call x1, Pallas kernels, on_device(): pl.pallas_call(finish, out_shape=(rows, rows, rows, rates_shape, jax.Shap...  2.51 us

profile of v3, /device:TPU:1, one launch (start us, length us, event | category | flops | bytes accessed | tf_op | source)
XLA Modules:
  0.0 106.6 jit_solution(9813337951756481801)
XLA Ops:
  0.6 103.4 %layer_grad.1 = (bf16[3,128,768]{2,1,0:T(8,128)(2,1)}, f32[4,128]{1,0:T(4,128)}, f32[3,8,256]{2,1,0:T(8,128)}) custom-call(bf16[128,768]{1,0:T(8,128)(2,1)} %q_hbm.1, bf16[128,768]{1,0:T(8,128)(2,1)} %k_hbm.1, bf16[128,768]{1,0:T(8,128)(2,1)} %v_hbm.1, f32[4,128]{1,0:T(4,128)} %bitcast.3, bf16[128,768]{1,0:T(8,128)(2,1)} %g_hbm.1, f32[192,4608]{1,0:T(8,128)} %w_hbm.1), custom_call_target="tpu_custom_call" | custom-call | tf_op jit(solution)/shard_map/layer_grad/pallas_call | solution.py:729
  104.0 2.5 %outputs.1 = (bf16[128,768]{1,0:T(8,128)(2,1)}, bf16[128,768]{1,0:T(8,128)(2,1)}, bf16[128,768]{1,0:T(8,128)(2,1)}, f32[4,128]{1,0:T(4,128)}, f32[18,192]{1,0:T(8,128)}) custom-call(bf16[3,128,768]{2,1,0:T(8,128)(2,1)} %get-tuple-element.13.rows, f32[4,128]{1,0:T(4,128)} %get-tuple-element.14.rate_rows, f32[3,8,256]{2,1,0:T(8,128)} %get-tuple-element.15.groups), custom_call_target="tpu_custom_call" | custom-call | tf_op jit(solution)/shard_map/outputs/pallas_call | solution.py:745

commit v4 on v3

--- a/solution.py
+++ b/solution.py
@@ -23,7 +23,7 @@
 CHUNK = 256
 TOTAL_ROWS = ROWS * NX * NY * NZ * 2
 COEFFICIENT = step_size * math.sqrt(TOTAL_ROWS)
-N_SEMS = 240
+N_SEMS = 64
 GROUP = 6
 
 
@@ -37,7 +37,7 @@
 ROW_TILES = UNITS // 8
 PIECE = UNITS // NX
 
-PARTS = (("x", (0, 1, 2)), ("z", (3, 4)))
+PARTS = (("x", (0, 1, 2, 3, 4)),)
 
 
 def part_sizes(part):
@@ -77,7 +77,6 @@
     s_ab_h, s_ab_l, e_ab_h, e_ab_l, s_c_h, s_c_l, e_c_h, e_c_l,
     acc_ab, acc_c, rate_rows, dq, xq, oq, rq, dkv, xkv, okv, rkv,
     p0_t, p0_r1, p0_s1, p0_r2, p0_s2, p0_a1, p0_f1, p0_g,
-    p1_t, p1_r1, p1_s1, p1_r2, p1_s2, p1_a1, p1_f1, p1_g,
     f_t, f_r1, f_s1, f_r2, d_grp, f_msg,
     send_sems, recv_sems, far_sems, load_sems,
 ):
@@ -113,12 +112,13 @@
     barrier = pltpu.get_barrier_semaphore()
     peers = [("x", d) for d in range(1, NX)] + [("z", d) for d in range(1, NZ)]
     peers += [("y", d) for d in range(1, NY)] + [("core", 1)]
-    for axis, offset in peers:
-        pl.semaphore_signal(barrier, inc=1, device_id=peer(axis, offset), device_id_type=MESH)
     for t in range(3):
         @pl.when(near_index[t] != mine)
         def _():
             pl.semaphore_signal(barrier, inc=1, device_id=device(*near_source[t]), device_id_type=MESH)
+    peers = sorted(peers, key=lambda one: one[0], reverse=True)
+    for axis, offset in peers:
+        pl.semaphore_signal(barrier, inc=1, device_id=peer(axis, offset), device_id_type=MESH)
 
     ids = itertools.count()
     started = []
@@ -132,6 +132,30 @@
         copy.start()
         started.append(copy)
         return copy
+
+    def send_all(triples, all_of_them):
+        which = next(ids)
+        for src, dst, target in triples:
+            copy = pltpu.make_async_remote_copy(
+                src_ref=src, dst_ref=dst, send_sem=send_sems.at[which], recv_sem=recv_sems.at[which],
+                device_id=target, device_id_type=MESH,
+            )
+            copy.start()
+        whole = pltpu.make_async_remote_copy(
+            src_ref=all_of_them, dst_ref=all_of_them, send_sem=send_sems.at[which], recv_sem=recv_sems.at[which],
+            device_id=target, device_id_type=MESH,
+        )
+        started.append(whole)
+        return whole
+
+    def take_started():
+        taken = list(started)
+        started.clear()
+        return taken
+
+    def drain(copies):
+        for copy in copies:
+            copy.wait_send()
 
     row_loads = []
     for n, (src, dst) in enumerate(((k_hbm, k_ref), (v_hbm, v_ref), (q_hbm, q_ref), (g_hbm, g_ref))):
@@ -229,12 +253,17 @@
 
     GATE, UP = slice(0, PAD), slice(PAD, 2 * PAD)
 
-    def add_terms(b, rows, gate_term, up_term, pull_term, left, right):
-        s_ab_h[b, rows, GATE], s_ab_l[b, rows, GATE] = split(gate_term)
-        s_ab_h[b, rows, UP], s_ab_l[b, rows, UP] = split(up_term)
-        s_c_h[b, rows, :], s_c_l[b, rows, :] = split(pull_term)
-        acc_ab[b] += tn(s_ab_h[b, rows, :], left) + tn(s_ab_l[b, rows, :], left)
-        acc_c[b] += tn(s_c_h[b, rows, :], right) + tn(s_c_l[b, rows, :], right)
+    def add_terms(b, rows, gate_term, up_term, pull_term, left, right, passes=2):
+        both = jnp.concatenate([gate_term, up_term], axis=1)
+        both_h, both_l = split(both)
+        pull_h, pull_l = split(pull_term)
+        s_ab_h[b, rows, :], s_c_h[b, rows, :] = both_h, pull_h
+        s_ab_l[b, rows, :], s_c_l[b, rows, :] = both_l, pull_l
+        both_sum, pull_sum = tn(both_h, left), tn(pull_h, right)
+        if passes == 2:
+            both_sum, pull_sum = both_sum + tn(both_l, left), pull_sum + tn(pull_l, right)
+        acc_ab[b] += both_sum
+        acc_c[b] += pull_sum
 
     def update_chunk(b, i):
         rows = slice(i * CHUNK, (i + 1) * CHUNK)
@@ -283,10 +312,7 @@
     rate_sum = sum(kv[s, ROWS:ROWS + 8, 0:ROWS] for s in range(SLOTS))
     total_part = jnp.sum(rate_sum[0:1, :], axis=1, keepdims=True)
 
-    parts = (
-        (p0_t, p0_r1, p0_s1, p0_r2, p0_s2, p0_a1, p0_f1, p0_g),
-        (p1_t, p1_r1, p1_s1, p1_r2, p1_s2, p1_a1, p1_f1, p1_g),
-    )
+    parts = ((p0_t, p0_r1, p0_s1, p0_r2, p0_s2, p0_a1, p0_f1, p0_g),)
 
     def lanes_of(first, second, third, tail):
         return (
@@ -308,11 +334,12 @@
         t = parts[p][0]
         for jj, j in enumerate(lane_tiles):
             t[r, jj * ROW_TILES:(jj + 1) * ROW_TILES] = source[j].reshape(ROW_TILES, 8, 128)
-        copies = []
+        r1 = parts[p][1]
+        triples = []
         for d in range(1, first):
             there = (place[axis] + d) % first
-            copies.append(send(t.at[r, pl.ds(there * shard, shard)], parts[p][1].at[r, d - 1], peer(axis, d)))
-        return copies
+            triples.append((t.at[r, pl.ds(there * shard, shard)], r1.at[r, d - 1], peer(axis, d)))
+        return send_all(triples, r1.at[r])
 
     def start_of(p, k):
         _, second, shard, window = part_sizes(PARTS[p])
@@ -324,26 +351,26 @@
         first, second, shard, window = part_sizes(PARTS[p])
         t, r1, s1, r2 = parts[p][:4]
         total = t[r, pl.ds(place[axis] * shard, shard)]
+        copies.wait_recv()
         for d in range(1, first):
-            copies[d - 1].wait_recv()
             total = total + r1[r, d - 1]
         s1[r] = total
-        out = []
+        triples = []
         for d in range(1, second):
             there = (place[other] + d) % second
-            out.append(send(s1.at[r, pl.ds(start_of(p, there), window)], r2.at[r, d - 1], peer(other, d)))
-        return out
+            triples.append((s1.at[r, pl.ds(start_of(p, there), window)], r2.at[r, d - 1], peer(other, d)))
+        return send_all(triples, r2.at[r])
 
     def third_stage(r, p, copies):
         other = "z" if PARTS[p][0] == "x" else "x"
         _, second, shard, window = part_sizes(PARTS[p])
         _, _, s1, r2, s2, a1, f1, _ = parts[p]
         total = s1[r, pl.ds(start_of(p, place[other]), window)]
+        copies.wait_recv()
         for d in range(1, second):
-            copies[d - 1].wait_recv()
             total = total + r2[r, d - 1]
         s2[r] = total
-        return [send(s2.at[r], a1.at[r, d - 1], peer(other, d)) for d in range(1, second)]
+        return send_all([(s2.at[r], a1.at[r, d - 1], peer(other, d)) for d in range(1, second)], a1.at[r])
 
     def fourth_stage(r, p, copies):
         axis = PARTS[p][0]
@@ -351,12 +378,12 @@
         first, second, shard, window = part_sizes(PARTS[p])
         _, _, _, _, s2, a1, f1, g = parts[p]
         f1[r, pl.ds(start_of(p, place[other]), window)] = s2[r]
+        copies.wait_recv()
         for d in range(1, second):
-            copies[d - 1].wait_recv()
             there = (place[other] + second - d) % second
             f1[r, pl.ds(start_of(p, there), window)] = a1[r, d - 1]
         here = pl.ds(place[axis] * shard, shard)
-        out = [send(f1.at[r], g.at[r, here], peer(axis, d)) for d in range(1, first)]
+        out = send_all([(f1.at[r], g.at[r, here], peer(axis, d)) for d in range(1, first)], parts[p][1].at[r])
         g[r, here] = f1[r]
         return out
 
@@ -367,17 +394,16 @@
 
         def start(self, tail):
             source = sums_of(self.b, tail)
-            self.copies = [start_stage(self.r, p, source) for p in (1, 0)][::-1]
+            self.copies = [start_stage(self.r, p, source) for p in range(len(PARTS))]
 
         def step(self, stage):
-            self.copies = [stage(self.r, p, self.copies[p]) for p in range(2)]
+            self.copies = [stage(self.r, p, self.copies[p]) for p in range(len(PARTS))]
 
         def result(self):
             for group in self.copies:
-                for copy in group:
-                    copy.wait_recv()
+                group.wait_recv()
             tiles = {}
-            for p in range(2):
+            for p in range(len(PARTS)):
                 for jj, j in enumerate(PARTS[p][1]):
                     tiles[j] = parts[p][7][self.r, jj * ROW_TILES:(jj + 1) * ROW_TILES].reshape(UNITS, 128)
             gate = jnp.concatenate([tiles[0], tiles[2][:, 0:64]], axis=1)
@@ -457,6 +483,7 @@
         lax.fori_loop(0, ALL_ROWS // CHUNK, apply_chunk, 0)
 
     new_sums = [Sum(1, b) for b in range(BLOCKS)]
+    early = take_started()
     for b in range(BLOCKS):
         with jax.named_scope("apply"):
             totals, scale = new_weights(b)
@@ -495,6 +522,7 @@
     query_pair = send(dq.at[pl.ds(4, 4)], xq, peer("core", 1))
     new_sums[0].step(third_stage)
     query_back = return_rows(query_pair, dq, xq, oq, rq)
+    drain(early)
     new_sums[1].step(third_stage)
     for b in range(BLOCKS):
         new_sums[b].step(fourth_stage)
@@ -527,7 +555,7 @@
             c_gate = one * m1[b, rows, :] + two * by_two + three * by_slope
             c_up = one * by_two + three * by_act
             c_pull = one * by_slope + two * by_act
-            add_terms(b, rows, c_gate, c_up, c_pull, keys, values)
+            add_terms(b, rows, c_gate, c_up, c_pull, keys, values, passes=1)
             by_rate = c_pull * pull_s[b, rows, :] + three * (by_act * up_s[b, rows, :])
             by_rate_h, by_rate_l = split(by_rate * inv_rates[rows, :])
             ones = jnp.ones((8, PAD), bf16)
@@ -537,6 +565,7 @@
 
         lax.fori_loop(0, ALL_ROWS // CHUNK, pull_chunk, 0)
 
+    early = take_started()
     weight_copies = []
     d_totals = jnp.zeros((1, 1), f32)
     for b in range(BLOCKS):
@@ -546,9 +575,11 @@
             tiles = sums_of(b, jnp.zeros((UNITS, 64), f32))
             for j in range(5):
                 f_t[b, :, 128 * j:128 * (j + 1)] = tiles[j]
+            triples = []
             for d in range(1, NX):
                 first = pl.multiple_of(((x + d) % NX) * PIECE, PIECE)
-                weight_copies.append(send(f_t.at[b, pl.ds(first, PIECE)], f_r1.at[b, d - 1], peer("x", d)))
+                triples.append((f_t.at[b, pl.ds(first, PIECE)], f_r1.at[b, d - 1], peer("x", d)))
+            weight_copies.append(send_all(triples, f_r1.at[b]))
 
     def key_chunk(i, _):
         rows = pl.ds(pl.multiple_of(i * ROWS, ROWS), ROWS)
@@ -574,13 +605,14 @@
     with jax.named_scope("x_sums"):
         for b in range(BLOCKS):
             total = f_t[b, pl.ds(pl.multiple_of(x * PIECE, PIECE), PIECE), :]
+            weight_copies[b].wait_recv()
             for d in range(1, NX):
-                weight_copies[(NX - 1) * b + d - 1].wait_recv()
                 total = total + f_r1[b, d - 1]
             for n in range(4):
                 f_s1[4 * b + n, 0:GROUP, :] = total[GROUP * n:GROUP * (n + 1), :]
                 f_s1[4 * b + n, GROUP:8, :] = jnp.zeros((8 - GROUP, 640), f32)
-        weight_copies = [send(f_s1.at[(z + d) % NZ], f_r2.at[d - 1], peer("z", d)) for d in range(1, NZ)]
+        triples = [(f_s1.at[(z + d) % NZ], f_r2.at[d - 1], peer("z", d)) for d in range(1, NZ)]
+        weight_copies = send_all(triples, f_r2)
     with jax.named_scope("row_returns"):
         row_back = return_rows(pair, dkv, xkv, okv, rkv)
     with jax.named_scope("direct"):
@@ -591,11 +623,12 @@
                     group = 8 * (n // 4) + 4 * b + n % 4
                     d_grp[group, 0:GROUP, 128 * j:128 * (j + 1)] = tiles[j][GROUP * n:GROUP * (n + 1), :]
 
+    drain(early)
     z_scope = jax.named_scope("z_sums")
     z_scope.__enter__()
     total = f_s1[z]
+    weight_copies.wait_recv()
     for d in range(1, NZ):
-        weight_copies[d - 1].wait_recv()
         total = total + f_r2[d - 1]
     total = (total + d_grp[8 * x + z]) * (1.0 / math.sqrt(TOTAL_ROWS))
     for m, (low, high) in enumerate(((0, 256), (128, 320), (384, 512))):
@@ -651,8 +684,7 @@
             @pl.when(far_owner[m] != mine)
             def _():
                 far_copies[m].wait_send()
-        for copy in started:
-            copy.wait_send()
+        drain(started)
 
 
 def finish(rows, rate_rows, groups, query_out, key_out, value_out, rate_out, fast_out, sems):

time: 107 us -> 101 us (0.944)
  Pallas kernels: 106 us -> 99.8 us
    pallas_call x1, Pallas kernels: 103 us -> 97.3 us  [on_device(): pl.pallas_call(kernel, out_shape=(jax.ShapeDtypeStruct((3, ROWS, HEADS *...]
where the time goes in v4:
time: 101 us; the launch traced here: 100 us
  Pallas kernels  99.8 us (99%)
    pallas_call x1, Pallas kernels, on_device(): pl.pallas_call(kernel, out_shape=(jax.ShapeDtypeStruct((3, ROWS, HEADS *...  97.3 us
    pallas_call x1, Pallas kernels, on_device(): pl.pallas_call(finish, out_shape=(rows, rows, rows, rates_shape, jax.Shap...  2.51 us

profile of v4, /device:TPU:1, one launch (start us, length us, event | category | flops | bytes accessed | tf_op | source)
XLA Modules:
  0.0 100.4 jit_solution(2896152596171101669)
XLA Ops:
  0.6 97.3 %layer_grad.1 = (bf16[3,128,768]{2,1,0:T(8,128)(2,1)}, f32[4,128]{1,0:T(4,128)}, f32[3,8,256]{2,1,0:T(8,128)}) custom-call(bf16[128,768]{1,0:T(8,128)(2,1)} %q_hbm.1, bf16[128,768]{1,0:T(8,128)(2,1)} %k_hbm.1, bf16[128,768]{1,0:T(8,128)(2,1)} %v_hbm.1, f32[4,128]{1,0:T(4,128)} %bitcast.3, bf16[128,768]{1,0:T(8,128)(2,1)} %g_hbm.1, f32[192,4608]{1,0:T(8,128)} %w_hbm.1), custom_call_target="tpu_custom_call" | custom-call | tf_op jit(solution)/shard_map/layer_grad/pallas_call | solution.py:761
  97.9 2.5 %outputs.1 = (bf16[128,768]{1,0:T(8,128)(2,1)}, bf16[128,768]{1,0:T(8,128)(2,1)}, bf16[128,768]{1,0:T(8,128)(2,1)}, f32[4,128]{1,0:T(4,128)}, f32[18,192]{1,0:T(8,128)}) custom-call(bf16[3,128,768]{2,1,0:T(8,128)(2,1)} %get-tuple-element.13.rows, f32[4,128]{1,0:T(4,128)} %get-tuple-element.14.rate_rows, f32[3,8,256]{2,1,0:T(8,128)} %get-tuple-element.15.groups), custom_call_target="tpu_custom_call" | custom-call | tf_op jit(solution)/shard_map/outputs/pallas_call | solution.py:777

commit v5 on v4

--- a/solution.py
+++ b/solution.py
@@ -21,6 +21,7 @@
 SLOTS = 8
 ALL_ROWS = SLOTS * ROWS
 CHUNK = 256
+WIDE = 512
 TOTAL_ROWS = ROWS * NX * NY * NZ * 2
 COEFFICIENT = step_size * math.sqrt(TOTAL_ROWS)
 N_SEMS = 64
@@ -28,7 +29,7 @@
 
 
 def device(x, y, z, core):
-    return ((x // 2) * 2 + core, (y * 2 + x % 2) * 8 + z)
+    return (lax.div(x, 2) * 2 + core, (y * 2 + lax.rem(x, 2)) * 8 + z)
 
 
 BLOCKS = 2
@@ -68,9 +69,9 @@
 
 
 def kernel(
-    q_hbm, k_hbm, v_hbm, r_ref, g_hbm, w_hbm,
+    q_hbm, k_hbm, v_hbm, r_hbm, g_hbm, w_hbm,
     rows_ref, rg_out, fg_out,
-    q_ref, k_ref, v_ref, g_ref,
+    q_ref, k_ref, v_ref, g_ref, r_ref,
     w_load, w_own, wh_ab, wl_ab, nh_ab, nl_ab, wh_c, wl_c, nh_c, nl_c, moved, gm, norms,
     kv_send, qg_send, kv, qg, rates, inv_rates, kb, vb, qb, gb,
     gate_s, up_s, pull_s, m1, m2, m3, m4,
@@ -86,14 +87,20 @@
     mine = view * 64 + patch
     half_block = 2 * y + core
 
+    known = {}
+
     def peer(axis, offset):
-        if axis == "x":
-            return device((x + offset) % NX, y, z, core)
-        if axis == "y":
-            return device(x, (y + offset) % NY, z, core)
-        if axis == "z":
-            return device(x, y, (z + offset) % NZ, core)
-        return device(x, y, z, 1 - core)
+        if (axis, offset) not in known:
+            if axis == "x":
+                target = device(lax.rem(x + offset, NX), y, z, core)
+            elif axis == "y":
+                target = device(x, lax.rem(y + offset, NY), z, core)
+            elif axis == "z":
+                target = device(x, y, lax.rem(z + offset, NZ), core)
+            else:
+                target = device(x, y, z, 1 - core)
+            known[axis, offset] = target
+        return known[axis, offset]
 
     place = {"x": x, "z": z}
 
@@ -158,7 +165,7 @@
             copy.wait_send()
 
     row_loads = []
-    for n, (src, dst) in enumerate(((k_hbm, k_ref), (v_hbm, v_ref), (q_hbm, q_ref), (g_hbm, g_ref))):
+    for n, (src, dst) in enumerate(((k_hbm, k_ref), (v_hbm, v_ref), (r_hbm, r_ref), (q_hbm, q_ref), (g_hbm, g_ref))):
         load = pltpu.make_async_copy(src, dst, load_sems.at[3 + n])
         load.start()
         row_loads.append(load)
@@ -175,8 +182,8 @@
             buffer[h, 0:ROWS, 0:HD] = left[:, cols].astype(f32)
             buffer[h, 0:ROWS, HD:2 * HD] = right[:, cols].astype(f32)
 
-    row_loads[0].wait()
-    row_loads[1].wait()
+    for load in row_loads[:3]:
+        load.wait()
     pack(kv_send, k_ref, v_ref)
     for h in range(HEADS):
         kv_send[h, ROWS:ROWS + 8, :] = jnp.zeros((8, 2 * HD), f32)
@@ -193,8 +200,8 @@
         return out
 
     kv_copies = scatter_heads(kv_send, kv)
-    row_loads[2].wait()
-    row_loads[3].wait()
+    for load in row_loads[3:]:
+        load.wait()
     pack(qg_send, q_ref, g_ref)
 
     def store_weights(ab_h, ab_l, c_h, c_l, b, m, value):
@@ -253,17 +260,14 @@
 
     GATE, UP = slice(0, PAD), slice(PAD, 2 * PAD)
 
-    def add_terms(b, rows, gate_term, up_term, pull_term, left, right, passes=2):
+    def add_terms(b, rows, gate_term, up_term, pull_term, left, right):
         both = jnp.concatenate([gate_term, up_term], axis=1)
         both_h, both_l = split(both)
         pull_h, pull_l = split(pull_term)
         s_ab_h[b, rows, :], s_c_h[b, rows, :] = both_h, pull_h
         s_ab_l[b, rows, :], s_c_l[b, rows, :] = both_l, pull_l
-        both_sum, pull_sum = tn(both_h, left), tn(pull_h, right)
-        if passes == 2:
-            both_sum, pull_sum = both_sum + tn(both_l, left), pull_sum + tn(pull_l, right)
-        acc_ab[b] += both_sum
-        acc_c[b] += pull_sum
+        acc_ab[b] += tn(both_h, left) + tn(both_l, left)
+        acc_c[b] += tn(pull_h, right) + tn(pull_l, right)
 
     def update_chunk(b, i):
         rows = slice(i * CHUNK, (i + 1) * CHUNK)
@@ -337,13 +341,13 @@
         r1 = parts[p][1]
         triples = []
         for d in range(1, first):
-            there = (place[axis] + d) % first
+            there = lax.rem(place[axis] + d, first)
             triples.append((t.at[r, pl.ds(there * shard, shard)], r1.at[r, d - 1], peer(axis, d)))
         return send_all(triples, r1.at[r])
 
     def start_of(p, k):
         _, second, shard, window = part_sizes(PARTS[p])
-        return ((shard - window) * k) // (second - 1)
+        return lax.div((shard - window) * k, second - 1)
 
     def second_stage(r, p, copies):
         axis = PARTS[p][0]
@@ -357,7 +361,7 @@
         s1[r] = total
         triples = []
         for d in range(1, second):
-            there = (place[other] + d) % second
+            there = lax.rem(place[other] + d, second)
             triples.append((s1.at[r, pl.ds(start_of(p, there), window)], r2.at[r, d - 1], peer(other, d)))
         return send_all(triples, r2.at[r])
 
@@ -380,7 +384,7 @@
         f1[r, pl.ds(start_of(p, place[other]), window)] = s2[r]
         copies.wait_recv()
         for d in range(1, second):
-            there = (place[other] + second - d) % second
+            there = lax.rem(place[other] + second - d, second)
             f1[r, pl.ds(start_of(p, there), window)] = a1[r, d - 1]
         here = pl.ds(place[axis] * shard, shard)
         out = send_all([(f1.at[r], g.at[r, here], peer(axis, d)) for d in range(1, first)], parts[p][1].at[r])
@@ -471,7 +475,7 @@
 
     def apply_block(b):
         def apply_chunk(i, _):
-            rows = pl.ds(pl.multiple_of(i * CHUNK, CHUNK), CHUNK)
+            rows = pl.ds(pl.multiple_of(i * WIDE, WIDE), WIDE)
             queries, grads = qb[rows, :], gb[rows, :]
             both = nt(queries, nh_ab[b]) + nt(queries, nl_ab[b])
             gate, up = both[:, GATE], both[:, UP]
@@ -480,7 +484,7 @@
             add_terms(b, rows, pulled * up * slope, pulled * act, act * up, queries, grads)
             return 0
 
-        lax.fori_loop(0, ALL_ROWS // CHUNK, apply_chunk, 0)
+        lax.fori_loop(0, ALL_ROWS // WIDE, apply_chunk, 0)
 
     new_sums = [Sum(1, b) for b in range(BLOCKS)]
     early = take_started()
@@ -496,13 +500,13 @@
 
     def query_grads(b):
         def query_chunk(i, _):
-            rows = pl.ds(pl.multiple_of(i * ROWS, ROWS), ROWS)
-            slot = (i % 2) * 4 + i // 2
+            rows = pl.ds(pl.multiple_of(i * CHUNK, CHUNK), CHUNK)
             part = product(s_ab_h.at[b], s_ab_l.at[b], nh_ab[b], nl_ab[b], rows)
-            dq[slot] = part if b == 0 else dq[slot] + part
+            dq[i] = part[0:ROWS] if b == 0 else dq[i] + part[0:ROWS]
+            dq[4 + i] = part[ROWS:CHUNK] if b == 0 else dq[4 + i] + part[ROWS:CHUNK]
             return 0
 
-        lax.fori_loop(0, SLOTS, query_chunk, 0)
+        lax.fori_loop(0, 4, query_chunk, 0)
 
     def return_rows(pair, partial, arrived, sums, landing):
         pair.wait_recv()
@@ -546,7 +550,7 @@
 
     def pull_block(b):
         def pull_chunk(i, _):
-            rows = pl.ds(pl.multiple_of(i * CHUNK, CHUNK), CHUNK)
+            rows = pl.ds(pl.multiple_of(i * WIDE, WIDE), WIDE)
             keys, values = kb[rows, :], vb[rows, :]
             both = nt(keys, nh_ab[b]) + nt(keys, nl_ab[b])
             one, two = both[:, GATE], both[:, UP]
@@ -555,7 +559,7 @@
             c_gate = one * m1[b, rows, :] + two * by_two + three * by_slope
             c_up = one * by_two + three * by_act
             c_pull = one * by_slope + two * by_act
-            add_terms(b, rows, c_gate, c_up, c_pull, keys, values, passes=1)
+            add_terms(b, rows, c_gate, c_up, c_pull, keys, values)
             by_rate = c_pull * pull_s[b, rows, :] + three * (by_act * up_s[b, rows, :])
             by_rate_h, by_rate_l = split(by_rate * inv_rates[rows, :])
             ones = jnp.ones((8, PAD), bf16)
@@ -563,7 +567,7 @@
             rate_rows[i] = part if b == 0 else rate_rows[i] + part
             return 0
 
-        lax.fori_loop(0, ALL_ROWS // CHUNK, pull_chunk, 0)
+        lax.fori_loop(0, ALL_ROWS // WIDE, pull_chunk, 0)
 
     early = take_started()
     weight_copies = []
@@ -582,24 +586,25 @@
             weight_copies.append(send_all(triples, f_r1.at[b]))
 
     def key_chunk(i, _):
-        rows = pl.ds(pl.multiple_of(i * ROWS, ROWS), ROWS)
-        slot = (i % 2) * 4 + i // 2
+        rows = pl.ds(pl.multiple_of(i * CHUNK, CHUNK), CHUNK)
         key_part, value_part = 0.0, 0.0
         for b in range(BLOCKS):
             key_part += product(s_ab_h.at[b], s_ab_l.at[b], wh_ab[b], wl_ab[b], rows)
             key_part += product(e_ab_h.at[b], e_ab_l.at[b], nh_ab[b], nl_ab[b], rows)
             value_part += product(s_c_h.at[b], s_c_l.at[b], wh_c[b], wl_c[b], rows)
             value_part += product(e_c_h.at[b], e_c_l.at[b], nh_c[b], nl_c[b], rows)
-        dkv[slot, 0:ROWS, 0:HD] = key_part
-        dkv[slot, 0:ROWS, HD:2 * HD] = value_part
+        for slot, first in ((i, 0), (4 + i, ROWS)):
+            dkv[slot, 0:ROWS, 0:HD] = key_part[first:first + ROWS]
+            dkv[slot, 0:ROWS, HD:2 * HD] = value_part[first:first + ROWS]
         return 0
 
     with jax.named_scope("row_grads"):
-        lax.fori_loop(0, SLOTS, key_chunk, 0)
+        lax.fori_loop(0, 4, key_chunk, 0)
         for s in range(SLOTS):
             dkv[s, ROWS:ROWS + 8, :] = jnp.zeros((8, 2 * HD), f32)
-            lane = (s // 4) * ROWS
-            dkv[s, ROWS:ROWS + 8, 0:ROWS] = rate_rows[s % 4, :, lane:lane + ROWS] + d_totals
+            first = row_block(s).start
+            lane = first % WIDE
+            dkv[s, ROWS:ROWS + 8, 0:ROWS] = rate_rows[first // WIDE, :, lane:lane + ROWS] + d_totals
         pair = send(dkv.at[pl.ds(4, 4)], xkv, peer("core", 1))
 
     with jax.named_scope("x_sums"):
@@ -705,6 +710,7 @@
     halves = (BLOCKS, ALL_ROWS)
     shapes = [
         *[pltpu.VMEM((ROWS, HEADS * HD), bf16)] * 4,
+        pltpu.VMEM((HEADS, ROWS), f32),
         pltpu.VMEM((3, HD, FF), f32),
         pltpu.VMEM((BLOCKS, 3, UNITS, HD), f32),
         *[pltpu.VMEM((BLOCKS, 2 * PAD, HD), bf16)] * 4,
@@ -720,7 +726,7 @@
         *[pltpu.VMEM(halves + (PAD,), bf16)] * 4,
         pltpu.VMEM((BLOCKS, 2 * PAD, HD), f32),
         pltpu.VMEM((BLOCKS, PAD, HD), f32),
-        pltpu.VMEM((ALL_ROWS // CHUNK, 8, CHUNK), f32),
+        pltpu.VMEM((ALL_ROWS // WIDE, 8, WIDE), f32),
         pltpu.VMEM((SLOTS, ROWS, HD), f32),
         *[pltpu.VMEM((4, ROWS, HD), f32)] * 3,
         pltpu.VMEM((SLOTS, ROWS + 8, 2 * HD), f32),
@@ -749,7 +755,7 @@
         pltpu.SemaphoreType.DMA((N_SEMS,)),
         pltpu.SemaphoreType.DMA((N_SEMS,)),
         pltpu.SemaphoreType.DMA((2, 3)),
-        pltpu.SemaphoreType.DMA((7,)),
+        pltpu.SemaphoreType.DMA((8,)),
     ]
     return shapes
 
@@ -757,6 +763,7 @@
 def on_device(queries, key_rows, value_rows, step_rates, fast_init, out_grad):
     vmem = pl.BlockSpec(memory_space=pltpu.VMEM)
     anywhere = pl.BlockSpec(memory_space=pl.ANY)
+    hbm = pl.BlockSpec(memory_space=pltpu.HBM)
     rates_shape = jax.ShapeDtypeStruct((HEADS, ROWS), f32)
     results = pl.pallas_call(
         kernel,
@@ -765,7 +772,7 @@
             rates_shape,
             jax.ShapeDtypeStruct((3, 8, 256), f32),
         ),
-        in_specs=[anywhere] * 3 + [vmem] + [anywhere] * 2,
+        in_specs=[hbm] * 6,
         out_specs=(vmem,) * 3,
         scratch_shapes=scratch(),
         compiler_params=pltpu.CompilerParams(
@@ -780,6 +787,7 @@
         in_specs=[vmem] * 3,
         out_specs=(anywhere,) * 3 + (vmem,) * 2,
         scratch_shapes=[pltpu.SemaphoreType.DMA((3,))],
+        compiler_params=pltpu.CompilerParams(vmem_limit_bytes=4 * 2**20),
         name="outputs",
     )(*results)
     return query_grad, key_grad, value_grad, rate_grad.T, fast_grad.T

time: 101 us -> 100 us (0.990)
  Pallas kernels: 99.8 us -> 97.1 us
  local copies, waits for them, and re-layouts: 0 us -> 2.46 us
    unnamed x0 -> x6, local copies, waits for them, and re-layouts: none -> 2.46 us
    pallas_call x1, Pallas kernels: 97.3 us -> 95.7 us  [on_device(): pl.pallas_call(kernel, out_shape=(jax.ShapeDtypeStruct((3, ROWS, HEADS *...]
    pallas_call x1, Pallas kernels: 2.51 us -> 1.44 us  [on_device(): pl.pallas_call(finish, out_shape=(rows, rows, rows, rates_shape, jax.Shap...]
where the time goes in v5:
time: 100 us
  Pallas kernels  97.1 us (97%)
  local copies, waits for them, and re-layouts  2.46 us (2%)
    pallas_call x1, Pallas kernels, on_device(): pl.pallas_call(kernel, out_shape=(jax.ShapeDtypeStruct((3, ROWS, HEADS *...  95.7 us
    unnamed x6, local copies, waits for them, and re-layouts  2.46 us

profile of v5, /device:TPU:1, one launch (start us, length us, event | category | flops | bytes accessed | tf_op | source)
XLA Modules:
  0.0 100.2 jit_solution(13376308060873046509)
XLA Ops:
  0.6 95.7 %layer_grad.1 = (bf16[3,128,768]{2,1,0:T(8,128)(2,1)}, f32[4,128]{1,0:T(4,128)}, f32[3,8,256]{2,1,0:T(8,128)}) custom-call(bf16[128,768]{1,0:T(8,128)(2,1)} %q_hbm.1, bf16[128,768]{1,0:T(8,128)(2,1)} %k_hbm.1, bf16[128,768]{1,0:T(8,128)(2,1)} %v_hbm.1, f32[4,128]{1,0:T(4,128)} %bitcast.3, bf16[128,768]{1,0:T(8,128)(2,1)} %g_hbm.1, f32[192,4608]{1,0:T(8,128)} %w_hbm.1), custom_call_target="tpu_custom_call" | custom-call | tf_op jit(solution)/shard_map/layer_grad/pallas_call | solution.py:768
  96.3 0.0 copy-start
  96.3 1.1 %copy-done = bf16[3,128,768]{2,1,0:T(8,128)(2,1)S(1)} copy-done((bf16[3,128,768]{2,1,0:T(8,128)(2,1)S(1)}, bf16[3,128,768]{2,1,0:T(8,128)(2,1)}, u32[]{:S(2)}) %copy-start) | copy-done | bytes 589848
  97.4 0.0 copy-start.1
  97.4 0.7 copy-done.1
  98.1 0.0 copy-start.2
  98.1 0.7 copy-done.2
  98.8 1.4 %outputs.1 = (bf16[128,768]{1,0:T(8,128)(2,1)}, bf16[128,768]{1,0:T(8,128)(2,1)}, bf16[128,768]{1,0:T(8,128)(2,1)}, f32[4,128]{1,0:T(4,128)}, f32[18,192]{1,0:T(8,128)}) custom-call(bf16[3,128,768]{2,1,0:T(8,128)(2,1)S(1)} %copy-done, f32[4,128]{1,0:T(4,128)S(1)} %copy-done.2, f32[3,8,256]{2,1,0:T(8,128)S(1)} %copy-done.1), custom_call_target="tpu_custom_call" | custom-call | tf_op jit(solution)/shard_map/outputs/pallas_call | solution.py:784
Async XLA Ops:
  96.3 1.1 %copy-start = (bf16[3,128,768]{2,1,0:T(8,128)(2,1)S(1)}, bf16[3,128,768]{2,1,0:T(8,128)(2,1)}, u32[]{:S(2)}) copy-start(bf16[3,128,768]{2,1,0:T(8,128)(2,1)} %get-tuple-element.13.rows) | copy-start | bytes 1769476
  97.4 0.7 copy-start.1
  98.1 0.7 copy-start.2

commit v6 on v5

--- a/solution.py
+++ b/solution.py
@@ -70,7 +70,7 @@
 
 def kernel(
     q_hbm, k_hbm, v_hbm, r_hbm, g_hbm, w_hbm,
-    rows_ref, rg_out, fg_out,
+    rows_hbm, rg_out, fg_out,
     q_ref, k_ref, v_ref, g_ref, r_ref,
     w_load, w_own, wh_ab, wl_ab, nh_ab, nl_ab, wh_c, wl_c, nh_c, nl_c, moved, gm, norms,
     kv_send, qg_send, kv, qg, rates, inv_rates, kb, vb, qb, gb,
@@ -79,7 +79,7 @@
     acc_ab, acc_c, rate_rows, dq, xq, oq, rq, dkv, xkv, okv, rkv,
     p0_t, p0_r1, p0_s1, p0_r2, p0_s2, p0_a1, p0_f1, p0_g,
     f_t, f_r1, f_s1, f_r2, d_grp, f_msg,
-    send_sems, recv_sems, far_sems, load_sems,
+    rows_ref, send_sems, recv_sems, far_sems, load_sems,
 ):
     view, patch = lax.axis_index("view"), lax.axis_index("patch")
     x, core = (view // 2) * 2 + (patch // 8) % 2, view % 2
@@ -664,6 +664,11 @@
         for h in range(HEADS):
             d = (h + NY - y) % NY
             rows_ref[which, :, HD * h:HD * (h + 1)] = landing[d, 0:ROWS, lanes:lanes + HD].astype(bf16)
+        store = pltpu.make_async_copy(rows_ref.at[which], rows_hbm.at[which], load_sems.at[8 + which])
+        store.start()
+        stores.append(store)
+
+    stores = []
 
     with jax.named_scope("query_rows"):
         for copy in query_back:
@@ -690,6 +695,8 @@
             def _():
                 far_copies[m].wait_send()
         drain(started)
+        for store in stores:
+            store.wait()
 
 
 def finish(rows, rate_rows, groups, query_out, key_out, value_out, rate_out, fast_out, sems):
@@ -752,10 +759,11 @@
         pltpu.VMEM((NZ - 1, 8, 640), f32),
         pltpu.VMEM((HALF // GROUP, 8, 640), f32),
         pltpu.VMEM((3, 8, 256), f32),
+        pltpu.VMEM((3, ROWS, HEADS * HD), bf16),
         pltpu.SemaphoreType.DMA((N_SEMS,)),
         pltpu.SemaphoreType.DMA((N_SEMS,)),
         pltpu.SemaphoreType.DMA((2, 3)),
-        pltpu.SemaphoreType.DMA((8,)),
+        pltpu.SemaphoreType.DMA((11,)),
     ]
     return shapes
 
@@ -773,7 +781,7 @@
             jax.ShapeDtypeStruct((3, 8, 256), f32),
         ),
         in_specs=[hbm] * 6,
-        out_specs=(vmem,) * 3,
+        out_specs=(anywhere, vmem, vmem),
         scratch_shapes=scratch(),
         compiler_params=pltpu.CompilerParams(
             collective_id=0, has_side_effects=True, vmem_limit_bytes=56 * 2**20
@@ -784,10 +792,9 @@
     query_grad, key_grad, value_grad, rate_grad, fast_grad = pl.pallas_call(
         finish,
         out_shape=(rows, rows, rows, rates_shape, jax.ShapeDtypeStruct((3 * GROUP, HD), f32)),
-        in_specs=[vmem] * 3,
+        in_specs=[anywhere, vmem, vmem],
         out_specs=(anywhere,) * 3 + (vmem,) * 2,
         scratch_shapes=[pltpu.SemaphoreType.DMA((3,))],
-        compiler_params=pltpu.CompilerParams(vmem_limit_bytes=4 * 2**20),
         name="outputs",
     )(*results)
     return query_grad, key_grad, value_grad, rate_grad.T, fast_grad.T

time: 100 us -> 117 us (1.17)
  Pallas kernels: 97.1 us -> 116 us
  local copies, waits for them, and re-layouts: 2.46 us -> 0 us
    pallas_call x1, Pallas kernels: 1.44 us -> 20.3 us  [on_device(): pl.pallas_call(finish, out_shape=(rows, rows, rows, rates_shape, jax.Shap...]
    unnamed x6 -> x0, local copies, waits for them, and re-layouts: 2.46 us -> none
where the time goes in v6:
time: 117 us; the launch traced here: 116 us
  Pallas kernels  116 us (99%)
    pallas_call x1, Pallas kernels, on_device(): pl.pallas_call(kernel, out_shape=(jax.ShapeDtypeStruct((3, ROWS, HEADS *...  95.5 us
    pallas_call x1, Pallas kernels, on_device(): pl.pallas_call(finish, out_shape=(rows, rows, rows, rates_shape, jax.Shap...  20.3 us

profile of v6, /device:TPU:1, one launch (start us, length us, event | category | flops | bytes accessed | tf_op | source)
XLA Modules:
  0.0 116.5 jit_solution(13192821112890181572)
XLA Ops:
  0.6 95.5 %layer_grad.1 = (bf16[3,128,768]{2,1,0:T(8,128)(2,1)}, f32[4,128]{1,0:T(4,128)}, f32[3,8,256]{2,1,0:T(8,128)}) custom-call(bf16[128,768]{1,0:T(8,128)(2,1)} %q_hbm.1, bf16[128,768]{1,0:T(8,128)(2,1)} %k_hbm.1, bf16[128,768]{1,0:T(8,128)(2,1)} %v_hbm.1, f32[4,128]{1,0:T(4,128)} %bitcast.3, bf16[128,768]{1,0:T(8,128)(2,1)} %g_hbm.1, f32[192,4608]{1,0:T(8,128)} %w_hbm.1), custom_call_target="tpu_custom_call" | custom-call | tf_op jit(solution)/shard_map/layer_grad/pallas_call | solution.py:776
  96.1 20.3 %outputs.1 = (bf16[128,768]{1,0:T(8,128)(2,1)}, bf16[128,768]{1,0:T(8,128)(2,1)}, bf16[128,768]{1,0:T(8,128)(2,1)}, f32[4,128]{1,0:T(4,128)}, f32[18,192]{1,0:T(8,128)}) custom-call(bf16[3,128,768]{2,1,0:T(8,128)(2,1)} %get-tuple-element.13.rows, f32[4,128]{1,0:T(4,128)} %get-tuple-element.14.rate_rows, f32[3,8,256]{2,1,0:T(8,128)} %get-tuple-element.15.groups), custom_call_target="tpu_custom_call" | custom-call | tf_op jit(solution)/shard_map/outputs/pallas_call | solution.py:792

commit v7 on v6

--- a/solution.py
+++ b/solution.py
@@ -792,7 +792,7 @@
     query_grad, key_grad, value_grad, rate_grad, fast_grad = pl.pallas_call(
         finish,
         out_shape=(rows, rows, rows, rates_shape, jax.ShapeDtypeStruct((3 * GROUP, HD), f32)),
-        in_specs=[anywhere, vmem, vmem],
+        in_specs=[vmem] * 3,
         out_specs=(anywhere,) * 3 + (vmem,) * 2,
         scratch_shapes=[pltpu.SemaphoreType.DMA((3,))],
         name="outputs",

time: 117 us -> 99.2 us (0.85)
  Pallas kernels: 116 us -> 98 us
    pallas_call x1, Pallas kernels: 20.3 us -> 2.51 us  [on_device(): pl.pallas_call(finish, out_shape=(rows, rows, rows, rates_shape, jax.Shap...]
where the time goes in v7:
time: 99.2 us; the launch traced here: 98.6 us
  Pallas kernels  98 us (99%)
    pallas_call x1, Pallas kernels, on_device(): pl.pallas_call(kernel, out_shape=(jax.ShapeDtypeStruct((3, ROWS, HEADS *...  95.5 us
    pallas_call x1, Pallas kernels, on_device(): pl.pallas_call(finish, out_shape=(rows, rows, rows, rates_shape, jax.Shap...  2.51 us

profile of v7, /device:TPU:1, one launch (start us, length us, event | category | flops | bytes accessed | tf_op | source)
XLA Modules:
  0.0 98.6 jit_solution(10102480319200338282)
XLA Ops:
  0.6 95.5 %layer_grad.1 = (bf16[3,128,768]{2,1,0:T(8,128)(2,1)}, f32[4,128]{1,0:T(4,128)}, f32[3,8,256]{2,1,0:T(8,128)}) custom-call(bf16[128,768]{1,0:T(8,128)(2,1)} %q_hbm.1, bf16[128,768]{1,0:T(8,128)(2,1)} %k_hbm.1, bf16[128,768]{1,0:T(8,128)(2,1)} %v_hbm.1, f32[4,128]{1,0:T(4,128)} %bitcast.3, bf16[128,768]{1,0:T(8,128)(2,1)} %g_hbm.1, f32[192,4608]{1,0:T(8,128)} %w_hbm.1), custom_call_target="tpu_custom_call" | custom-call | tf_op jit(solution)/shard_map/layer_grad/pallas_call | solution.py:776
  96.1 2.5 %outputs.1 = (bf16[128,768]{1,0:T(8,128)(2,1)}, bf16[128,768]{1,0:T(8,128)(2,1)}, bf16[128,768]{1,0:T(8,128)(2,1)}, f32[4,128]{1,0:T(4,128)}, f32[18,192]{1,0:T(8,128)}) custom-call(bf16[3,128,768]{2,1,0:T(8,128)(2,1)} %get-tuple-element.13.rows, f32[4,128]{1,0:T(4,128)} %get-tuple-element.14.rate_rows, f32[3,8,256]{2,1,0:T(8,128)} %get-tuple-element.15.groups), custom_call_target="tpu_custom_call" | custom-call | tf_op jit(solution)/shard_map/outputs/pallas_call | solution.py:792
